TPU v7x, 32 devices: a whole 2x2x4 slice. The times are simulated.
32 devices in a mesh: seq: 8 (over y, x, core), mp: 4 (over z).
Axes of the slice: x: 2, y: 2, z: 4, core: 2. Of those that a mesh axis runs over, the one named last changes fastest.
Arguments:
- byte_values: int32 [8192], P('seq'), may hold values from 0 to 255
- hash_owner: int32 [8192, 1], P('seq'), may hold values from 0 to 7; in each aligned block of 1024 rows (0 to 1023, 1024 to 2047, ...) at most 256 rows name the same one
- hash_slot: int32 [8192], P('seq'), may hold values from 0 to 4095
- patch_start: int32 [256], P('seq'), may hold values from 0 to 8191, as said below
- byte_table: bfloat16 [256, 1280], P(None, 'mp'), may hold values from -6 to 6
- hash_table: bfloat16 [32768, 1280], P('seq', 'mp'), may hold values from -6 to 6
- norm_gains: float32 [3, 1280], replicated, may hold values from 0.5 to 1.5
- w_query: bfloat16 [1280, 1280], P(None, 'mp'), may hold values from -8 to 8
- w_key: bfloat16 [1280, 1280], P(None, 'mp'), may hold values from -8 to 8
- w_value: bfloat16 [1280, 1280], P(None, 'mp'), may hold values from -0.15625 to 0.15625
- w_attn_out: bfloat16 [1280, 1280], P('mp'), may hold values from -0.15625 to 0.15625
- w_gate: bfloat16 [1280, 3584], P('seq', 'mp'), may hold values from -0.15625 to 0.15625
- w_up: bfloat16 [1280, 3584], P('seq', 'mp'), may hold values from -0.15625 to 0.15625
- w_down: bfloat16 [3584, 1280], P('mp', 'seq'), may hold values from -0.09375 to 0.09375
- w_cross_query: bfloat16 [1280, 1280], P(None, 'mp'), may hold values from -8 to 8
- w_cross_key: bfloat16 [1280, 1280], P(None, 'mp'), may hold values from -8 to 8
- w_cross_value: bfloat16 [1280, 1280], P(None, 'mp'), may hold values from -0.15625 to 0.15625
- w_cross_out: bfloat16 [1280, 1280], P('mp'), may hold values from -0.15625 to 0.15625
- w_global: bfloat16 [1280, 4096], P(None, 'mp'), may hold values from -0.15625 to 0.15625
Outputs:
- patches: bfloat16 [256, 4096], P('seq', 'mp')
Inputs may be any that keep to these rules, and one draw needn't show every extreme that they name: `hash_owner`: in each aligned block of 1024 rows (the bytes of one range) every value is named by at most 256 bytes; in some blocks one value is named by exactly 256 bytes. patch_start rises strictly and begins with 0. The patches p with p // 32 = s start at or after s * 1024 - 512 and end at or before (s + 1) * 1024 + 512; in every draw some group starts exactly 512 bytes before its range and some group ends exactly 512 bytes after its range.
All inputs are finite; a program needn't handle non-finite values.
Results may differ from a plain program's by a relative error of at most 0.025.
Values may be sent and summed in bfloat16 or wider, within the bound.
A program may use at most 128 MiB of HBM per device.

v0:
```python
import jax
import jax.numpy as jnp
from jax import lax
from jax.sharding import PartitionSpec as P

HD = 64
WINDOW = 512
REACH = 512


def passed_along(value, axis, steps):
    count = lax.axis_size(axis)
    first, last = (max(0, -steps), min(count, count - steps))
    return lax.ppermute(value, axis, [(source, source + steps) for source in range(first, last)])


def padded(cells, sides, width):
    for axis, dim in sides:
        count = lax.axis_size(axis)
        ends = count - 1
        head = lax.slice_in_dim(cells, 0, width, axis=dim)
        tail = lax.slice_in_dim(cells, cells.shape[dim] - width, cells.shape[dim], axis=dim)
        cells = jnp.concatenate(
            [
                lax.ppermute(tail, axis, [(i, (i + 1) % count) for i in range(ends)]),
                cells,
                lax.ppermute(head, axis, [((i + 1) % count, i) for i in range(ends)]),
            ],
            axis=dim,
        )
    return cells


def rms_scale(values, gain):
    return values * lax.rsqrt(jnp.mean(values * values, axis=-1, keepdims=True) + 1e-05) * gain


def masked_softmax(scores, valid):
    scores = jnp.where(valid, scores, -1e30)
    highest = jnp.max(scores, axis=-1, keepdims=True)
    raised = jnp.exp(scores - highest)
    return raised / jnp.sum(raised, axis=-1, keepdims=True)


def per_device(
    byte_values,
    hash_owner,
    hash_slot,
    patch_start,
    byte_table,
    hash_table,
    norm_gains,
    w_query,
    w_key,
    w_value,
    w_attn_out,
    w_gate,
    w_up,
    w_down,
    w_cross_query,
    w_cross_key,
    w_cross_value,
    w_cross_out,
    w_global,
):
    seq_count = lax.axis_size("seq")
    position = lax.axis_index("seq")
    length = byte_values.shape[0]
    local_width = w_query.shape[1]
    local_heads = local_width // HD
    capacity = 2 * length // seq_count
    owner = hash_owner[:, 0]
    owner_hot = (owner[:, None] == jnp.arange(seq_count, dtype=jnp.int32)[None, :]).astype(
        jnp.bfloat16
    )
    line = jnp.arange(length, dtype=jnp.int32)
    earlier = (line[:, None] > line[None, :]).astype(jnp.bfloat16)
    before = jnp.dot(earlier, owner_hot, preferred_element_type=jnp.float32)
    order = jnp.sum(before * owner_hot.astype(jnp.float32), axis=1).astype(jnp.int32)
    requests = jnp.zeros((seq_count, capacity), jnp.int32).at[owner, order].set(hash_slot)
    found = jnp.take(
        hash_table, lax.all_to_all(requests, "seq", split_axis=0, concat_axis=0, tiled=True), axis=0
    )
    fetched = lax.all_to_all(found, "seq", split_axis=0, concat_axis=0, tiled=True)
    hash_rows = fetched[owner, order]
    byte_hot = (byte_values[:, None] == jnp.arange(256, dtype=jnp.int32)[None, :]).astype(
        jnp.bfloat16
    )
    byte_rows = jnp.dot(byte_hot, byte_table, preferred_element_type=jnp.float32)
    embed = (byte_rows + hash_rows.astype(jnp.float32)).astype(jnp.bfloat16)
    residual = lax.all_to_all(embed, "mp", split_axis=0, concat_axis=1, tiled=True).astype(
        jnp.float32
    )
    normed = rms_scale(residual, norm_gains[0]).astype(jnp.bfloat16)
    layer_in = lax.all_gather(normed, "mp", axis=0, tiled=True)
    queries = jnp.dot(layer_in, w_query, preferred_element_type=jnp.float32).astype(jnp.bfloat16)
    keys = jnp.dot(layer_in, w_key, preferred_element_type=jnp.float32).astype(jnp.bfloat16)
    values = jnp.dot(layer_in, w_value, preferred_element_type=jnp.float32).astype(jnp.bfloat16)
    paired = jnp.stack([keys, values])
    earlier_pair = passed_along(paired[:, length - WINDOW :], "seq", 1)
    key_span = jnp.concatenate([earlier_pair[0], keys], axis=0)
    value_span = jnp.concatenate([earlier_pair[1], values], axis=0)
    first = position * length
    outputs = []
    for block in range(length // WINDOW):
        query_block = queries[block * WINDOW : (block + 1) * WINDOW].reshape(
            WINDOW, local_heads, HD
        )
        key_block = key_span[block * WINDOW : block * WINDOW + 2 * WINDOW].reshape(
            2 * WINDOW, local_heads, HD
        )
        value_block = value_span[block * WINDOW : block * WINDOW + 2 * WINDOW].reshape(
            2 * WINDOW, local_heads, HD
        )
        query_pos = first + block * WINDOW + jnp.arange(WINDOW, dtype=jnp.int32)
        key_pos = first + (block - 1) * WINDOW + jnp.arange(2 * WINDOW, dtype=jnp.int32)
        valid = (
            (key_pos[None, :] <= query_pos[:, None])
            & (key_pos[None, :] > query_pos[:, None] - WINDOW)
            & (key_pos[None, :] >= 0)
        )
        scores = jnp.einsum(
            "qhd,khd->hqk", query_block, key_block, preferred_element_type=jnp.float32
        ) * HD ** (-0.5)
        weights = masked_softmax(scores, valid[None]).astype(jnp.bfloat16)
        mixed_block = jnp.einsum(
            "hqk,khd->qhd", weights, value_block, preferred_element_type=jnp.float32
        ).astype(jnp.bfloat16)
        outputs.append(mixed_block.reshape(WINDOW, local_width))
    heads_out = jnp.concatenate(outputs, axis=0)
    residual = residual + lax.psum_scatter(
        jnp.dot(heads_out, w_attn_out, preferred_element_type=jnp.float32).astype(jnp.bfloat16),
        "mp",
        scatter_dimension=0,
        tiled=True,
    ).astype(jnp.float32)
    normed = rms_scale(residual, norm_gains[1]).astype(jnp.bfloat16)
    mlp_in = lax.all_gather(normed, "mp", axis=0, tiled=True)
    gate = jnp.dot(
        mlp_in,
        lax.all_gather(w_gate, "seq", axis=0, tiled=True),
        preferred_element_type=jnp.float32,
    )
    lifted = jnp.dot(
        mlp_in, lax.all_gather(w_up, "seq", axis=0, tiled=True), preferred_element_type=jnp.float32
    )
    hidden = (jax.nn.silu(gate) * lifted).astype(jnp.bfloat16)
    down_terms = jnp.dot(
        hidden,
        lax.all_gather(w_down, "seq", axis=1, tiled=True),
        preferred_element_type=jnp.float32,
    )
    residual = residual + lax.psum_scatter(
        down_terms.astype(jnp.bfloat16), "mp", scatter_dimension=0, tiled=True
    ).astype(jnp.float32)
    encoded = rms_scale(residual, norm_gains[2]).astype(jnp.bfloat16)
    states = lax.all_gather(encoded, "mp", axis=0, tiled=True)
    cross_keys = jnp.dot(states, w_cross_key, preferred_element_type=jnp.float32).astype(
        jnp.bfloat16
    )
    cross_values = jnp.dot(states, w_cross_value, preferred_element_type=jnp.float32).astype(
        jnp.bfloat16
    )
    following = passed_along(patch_start[:1], "seq", -1)
    last_end = jnp.where(position == seq_count - 1, seq_count * length, following[0])
    patch_end = jnp.concatenate([patch_start[1:], last_end[None]])
    patch_count = patch_start.shape[0]
    frame_states = padded(states, (("seq", 0),), REACH)
    margins = jnp.concatenate([frame_states[:REACH], frame_states[REACH + length :]], axis=0)
    margin_keys = jnp.dot(margins, w_cross_key, preferred_element_type=jnp.float32).astype(
        jnp.bfloat16
    )
    margin_values = jnp.dot(margins, w_cross_value, preferred_element_type=jnp.float32).astype(
        jnp.bfloat16
    )
    frame_keys = jnp.concatenate([margin_keys[:REACH], cross_keys, margin_keys[REACH:]], axis=0)
    frame_values = jnp.concatenate(
        [margin_values[:REACH], cross_values, margin_values[REACH:]], axis=0
    )
    frame_len = frame_states.shape[0]
    frame_pos = position * length - REACH + jnp.arange(frame_len, dtype=jnp.int32)
    member = (frame_pos[None, :] >= patch_start[:, None]) & (
        frame_pos[None, :] < patch_end[:, None]
    )
    counts = jnp.sum(member.astype(jnp.float32), axis=1)
    pooled = (
        jnp.dot(member.astype(jnp.bfloat16), frame_states, preferred_element_type=jnp.float32)
        / counts[:, None]
    )
    pooled_rows = pooled.astype(jnp.bfloat16)
    cross_queries = (
        jnp.dot(pooled_rows, w_cross_query, preferred_element_type=jnp.float32)
        .astype(jnp.bfloat16)
        .reshape(patch_count, local_heads, HD)
    )
    scores = jnp.einsum(
        "phd,khd->hpk",
        cross_queries,
        frame_keys.reshape(frame_len, local_heads, HD),
        preferred_element_type=jnp.float32,
    ) * HD ** (-0.5)
    weights = masked_softmax(scores, member[None]).astype(jnp.bfloat16)
    cross_heads = (
        jnp.einsum(
            "hpk,khd->phd",
            weights,
            frame_values.reshape(frame_len, local_heads, HD),
            preferred_element_type=jnp.float32,
        )
        .astype(jnp.bfloat16)
        .reshape(patch_count, local_width)
    )
    pooled, cross_heads = (pooled, cross_heads)
    mixed_patches = lax.psum(
        jnp.dot(cross_heads, w_cross_out, preferred_element_type=jnp.float32).astype(jnp.bfloat16),
        "mp",
    ).astype(jnp.float32)
    patch_hidden = (pooled + mixed_patches).astype(jnp.bfloat16)
    return jnp.dot(patch_hidden, w_global, preferred_element_type=jnp.float32).astype(jnp.bfloat16)


def solution(mesh):
    return jax.shard_map(
        per_device,
        mesh=mesh,
        in_specs=(
            P("seq"),
            P("seq", None),
            P("seq"),
            P("seq"),
            P(None, "mp"),
            P("seq", "mp"),
            P(),
            P(None, "mp"),
            P(None, "mp"),
            P(None, "mp"),
            P("mp", None),
            P("seq", "mp"),
            P("seq", "mp"),
            P("mp", "seq"),
            P(None, "mp"),
            P(None, "mp"),
            P(None, "mp"),
            P("mp", None),
            P(None, "mp"),
        ),
        out_specs=P("seq", "mp"),
        check_vma=False,
    )
```

profile of v0, /device:TPU:3, one launch (start us, length us, event | category | flops | bytes accessed | tf_op | source)
XLA Modules:
  0.0 580.9 jit_solution(18224280185250932194)
XLA Ops:
  7.4 1.3 fusion.35
  10.9 5.0 scatter_custom_fusion
  16.0 4.6 all-to-all-start
  20.5 4.5 copy.30
  25.1 11.1 %gather_fusion = bf16[2048,320]{1,0:T(8,128)(2,1)} fusion(bf16[4096,320]{1,0:T(8,128)(2,1)} %copy.30, s32[2048]{0:T(1024)S(1)} %broadcast_clamp_fusion), kind=kCustom, calls=%fused_computation | custom fusion | bytes 2629632 | tf_op jit(solution)/shard_map/jit(_take)/gather | solution.py:81
  36.3 2.5 copy.31
  38.8 1.4 broadcast_select_fusion
  40.3 20.6 %all_to_all.33 = bf16[8,256,320]{1,2,0:T(8,128)(2,1)} all-to-all(bf16[8,256,320]{1,2,0:T(8,128)(2,1)S(1)} %broadcast_select_fusion), channel_id=1, replica_groups=mesh['seq'=8,'mp'=4] {'seq'}, dimensions={0} | all-to-all | bytes 2621440 | tf_op jit(solution)/shard_map/all_to_all | solution.py:84
  60.8 2.6 copy.32
  63.4 13.4 %gather_fusion.1 = bf16[1024,320]{1,0:T(8,128)(2,1)S(1)} fusion(bf16[8,256,320]{2,1,0:T(8,128)(2,1)} %copy.32, s32[1024]{0:T(1024)S(1)} %bitcast.84), kind=kCustom, calls=%fused_computation.1 | custom fusion | bytes 1318912 | tf_op jit(solution)/shard_map/gather | solution.py:85
  78.0 1.6 fusion.30
  80.5 4.6 all-to-all-start.2
  85.2 16.8 %all-to-all-done.2 = bf16[4,256,320]{1,2,0:T(8,128)(2,1)S(1)} async-done(((bf16[4,256,320]{1,2,0:T(8,128)(2,1)}), bf16[4,256,320]{1,2,0:T(8,128)(2,1)S(1)}, u32[]{:S(2)}, u32[]{:S(2)}) %all-to-all-start.2) | async-done | bytes 655392 | tf_op jit(solution)/shard_map/all_to_all | solution.py:91
  102.2 1.5 multiply_convert_fusion.3
  103.8 1.4 and_and_fusion.1
  105.2 1.3 and_and_fusion
  106.5 51.3 %all-gather.7.cloned.1.call-done = bf16[1024,1280]{0,1:T(8,128)(2,1)} async-done(((bf16[256,1280]{0,1:T(8,128)(2,1)}), bf16[1024,1280]{0,1:T(8,128)(2,1)}) %all-gather.7.cloned.1.call-update) | async-done | bytes 2621456 | tf_op jit(solution)/shard_map/all_gather | solution.py:95
  157.8 3.1 convolution_convert_fusion.5
  163.0 3.6 collective-permute-start.1
  168.6 8.8 %fusion.58 = (f32[5,512]{1,0:T(8,128)S(1)}, f32[5,512,1024]{2,1,0:T(8,128)}) fusion(pred[512,1024]{1,0:T(8,128)(4,1)} %and_and_fusion, bf16[512,5,64]{0,2,1:T(8,128)(2,1)} %bitcast.98, bf16[1024,5,64]{0,2,1:T(8,128)(2,1)S(1)} %bitcast.91), kind=kOutput, calls=%fused_computation.134 | convolution fusion | flops 346031104 | bytes 12003328 | tf_op jit(solution)/shard_map/sub | solution.py:41
  177.3 6.7 %fusion.31 = bf16[5,64,512]{2,1,0:T(8,128)(2,1)} fusion(bf16[1024,5,64]{0,2,1:T(8,128)(2,1)} %bitcast.93, f32[5,512,1024]{2,1,0:T(8,128)} %get-tuple-element.24, f32[5,512]{1,0:T(8,128)S(1)} %get-tuple-element.23), kind=kOutput, calls=%fused_computation.64 | convolution fusion | flops 340951040 | bytes 11479040 | tf_op jit(solution)/shard_map/hqk,khd->qhd/dot_general | solution.py:126
  186.5 9.0 %fusion.59 = (f32[5,512]{1,0:T(8,128)S(1)}, f32[5,512,1024]{2,1,0:T(8,128)}) fusion(pred[512,1024]{1,0:T(8,128)(4,1)} %and_and_fusion.1, bf16[512,5,64]{0,2,1:T(8,128)(2,1)} %bitcast.97, bf16[1024,5,64]{0,2,1:T(8,128)(2,1)} %bitcast.96), kind=kOutput, calls=%fused_computation.135 | convolution fusion | flops 346031104 | bytes 12003328 | tf_op jit(solution)/shard_map/sub | solution.py:41
  195.5 5.8 %fusion.32 = bf16[5,64,512]{2,1,0:T(8,128)(2,1)S(1)} fusion(bf16[1024,5,64]{0,2,1:T(8,128)(2,1)S(1)} %bitcast.95, f32[5,512,1024]{2,1,0:T(8,128)} %get-tuple-element.26, f32[5,512]{1,0:T(8,128)S(1)} %get-tuple-element.25), kind=kOutput, calls=%fused_computation.65 | convolution fusion | flops 340951040 | bytes 11479040 | tf_op jit(solution)/shard_map/hqk,khd->qhd/dot_general | solution.py:126
  201.4 3.3 convolution_convert_fusion.1
  205.4 2.8 copy.35
  208.1 45.5 %reduce-scatter.3.cloned.1.call-done = bf16[256,1280]{1,0:T(8,128)(2,1)} async-done(((bf16[1024,1280]{1,0:T(8,128)(2,1)}), bf16[256,1280]{1,0:T(8,128)(2,1)}) %reduce-scatter.3.cloned.1.call-update) | async-done | bytes 655376 | tf_op jit(solution)/shard_map/reduce_scatter | solution.py:131
  253.6 1.9 multiply_reduce_fusion.1
  258.2 53.1 %all-gather.9.cloned.1.call-done = bf16[1024,1280]{1,0:T(8,128)(2,1)} async-done(((bf16[256,1280]{1,0:T(8,128)(2,1)}), bf16[1024,1280]{1,0:T(8,128)(2,1)}) %all-gather.9.cloned.1.call-update) | async-done | bytes 2621456 | tf_op jit(solution)/shard_map/all_gather | solution.py:138
  311.2 7.1 %fusion.61 = f32[1024,896]{1,0:T(8,128)} fusion(bf16[1024,1280]{1,0:T(8,128)(2,1)} %all-gather.9.cloned.1.call-done, bf16[1280,896]{1,0:T(8,128)(2,1)} %all-gather.11.cloned.1.call-done), kind=kOutput, calls=%fused_computation.137 | convolution fusion | flops 2348810240 | bytes 8585216 | tf_op jit(solution)/shard_map/dot_general | solution.py:139
  318.3 22.6 %all-gather.13.cloned.1.call-done = bf16[1280,896]{1,0:T(8,128)(2,1)} async-done(((bf16[160,896]{1,0:T(8,128)(2,1)}), bf16[1280,896]{1,0:T(8,128)(2,1)}) %all-gather.13.cloned.1.call-update) | async-done | bytes 2293776 | tf_op jit(solution)/shard_map/all_gather | solution.py:145
  340.9 30.5 %all-gather.15.cloned.1.call-done = bf16[896,1280]{0,1:T(8,128)(2,1)} async-done(((bf16[896,160]{0,1:T(8,128)(2,1)}), bf16[896,1280]{0,1:T(8,128)(2,1)}) %all-gather.15.cloned.1.call-update) | async-done | bytes 2293776 | tf_op jit(solution)/shard_map/all_gather | solution.py:150
  371.4 11.5 %convolution_convert_fusion = bf16[1024,1280]{1,0:T(8,128)(2,1)} fusion(bf16[896,1280]{0,1:T(8,128)(2,1)} %all-gather.15.cloned.1.call-done, f32[1024,896]{1,0:T(8,128)} %fusion.61, bf16[1024,1280]{1,0:T(8,128)(2,1)} %all-gather.9.cloned.1.call-done, bf16[1280,896]{1,0:T(8,128)(2,1)} %all-gather.13.cloned.1.call-done), kind=kOutput, calls=%fused_computation.32 | convolution fusion | flops 4704436224 | bytes 13500416 | tf_op jit(solution)/shard_map/dot_general | solution.py:148
  383.0 51.6 %reduce-scatter.5.cloned.1.call-done = bf16[256,1280]{1,0:T(8,128)(2,1)} async-done(((bf16[1024,1280]{1,0:T(8,128)(2,1)}), bf16[256,1280]{1,0:T(8,128)(2,1)}) %reduce-scatter.5.cloned.1.call-update) | async-done | bytes 655376 | tf_op jit(solution)/shard_map/reduce_scatter | solution.py:153
  434.6 2.0 multiply_reduce_fusion
  437.9 2.7 collective-permute-start
  440.7 2.9 collective-permute-done
  444.2 48.4 %all-gather.17.cloned.1.call-done = bf16[1024,1280]{1,0:T(8,128)(2,1)} async-done(((bf16[256,1280]{1,0:T(8,128)(2,1)}), bf16[1024,1280]{1,0:T(8,128)(2,1)}) %all-gather.17.cloned.1.call-update) | async-done | bytes 2621456 | tf_op jit(solution)/shard_map/all_gather | solution.py:157
  492.6 2.0 fusion.54
  494.6 3.7 collective-permute-start.2
  498.6 2.2 collective-permute-start.3
  501.0 1.9 convolution_convert_fusion.6
  502.9 1.9 convolution_convert_fusion.8
  504.8 19.0 %collective-permute-done.2 = bf16[512,1280]{1,0:T(8,128)(2,1)S(1)} collective-permute-done((bf16[512,1280]{1,0:T(8,128)(2,1)S(1)}, bf16[512,1280]{1,0:T(8,128)(2,1)S(1)}, u32[]{:S(2)}, u32[]{:S(2)}) %collective-permute-start.2) | collective-permute-done | bytes 1310752 | tf_op jit(solution)/shard_map/ppermute | solution.py:25
  523.9 4.7 collective-permute-done.3
  529.7 1.9 convolution_convert_fusion.9
  538.2 2.7 fusion.33
  542.0 29.5 %all-reduce.2.cloned.1.call-done = bf16[32,1280]{1,0:T(8,128)(2,1)} async-done(((bf16[32,1280]{1,0:T(8,128)(2,1)}), bf16[32,1280]{1,0:T(8,128)(2,1)}) %all-reduce.2.cloned.1.call-update) | async-done | bytes 81936 | tf_op jit(solution)/shard_map/psum | solution.py:214
  571.4 2.2 convolution_convert_fusion.10
  (120 shorter events, 24.8 us)
Async XLA Ops:
  7.4 564.1 %copy-start = (bf16[1280,1024]{1,0:T(8,128)(2,1)S(1)}, bf16[1280,1024]{1,0:T(8,128)(2,1)}, u32[]{:S(2)}) copy-start(bf16[1280,1024]{1,0:T(8,128)(2,1)} %param.37) | copy-start | bytes 7864324
  16.0 9.1 %all-to-all-start = ((s32[8,1,256]{2,1,0:T(1,128)}), s32[8,1,256]{2,1,0:T(1,128)S(1)}, u32[]{:S(2)}, u32[]{:S(2)}) async-start(s32[8,1,256]{2,1,0:T(1,128)} %bitcast.4), calls=%async_computation | async-start | bytes 16384 | tf_op jit(solution)/shard_map/all_to_all | solution.py:82
  63.4 14.6 %copy-start.16 = (s32[1024]{0:T(1024)S(1)}, s32[1024]{0:T(1024)}, u32[]{:S(2)}) copy-start(s32[1024]{0:T(1024)} %param.19) | copy-start | bytes 12292
  78.0 7.1 %copy-start.15 = (f32[3,1280]{1,0:T(4,128)S(1)}, f32[3,1280]{1,0:T(4,128)}, u32[]{:S(2)}) copy-start(f32[3,1280]{1,0:T(4,128)} %param.25) | copy-start | bytes 46084
  80.5 21.4 %all-to-all-start.2 = ((bf16[4,256,320]{1,2,0:T(8,128)(2,1)}), bf16[4,256,320]{1,2,0:T(8,128)(2,1)S(1)}, u32[]{:S(2)}, u32[]{:S(2)}) async-start(bf16[4,256,320]{1,2,0:T(8,128)(2,1)} %bitcast.88), calls=%async_computation.2 | async-start | bytes 1310720 | tf_op jit(solution)/shard_map/all_to_all | solution.py:91
  85.1 72.7 %all-gather.7.cloned.1.call-start = ((), (), s32[]{:S(2)}) async-start(), calls=%async_computation.5 | async-start | bytes 3276800 | tf_op jit(solution)/shard_map/all_gather | solution.py:95
  103.7 149.9 %reduce-scatter.3.cloned.1.call-start = ((), (), s32[]{:S(2)}) async-start(), calls=%async_computation.6 | async-start | bytes 3276800 | tf_op jit(solution)/shard_map/reduce_scatter | solution.py:131
  157.8 3.2 copy-start.18
  157.8 3.2 copy-start.19
  161.0 5.7 copy-start.20
  162.0 5.7 copy-start.6
  163.0 21.1 %collective-permute-start.1 = (bf16[2,512,320]{1,2,0:T(8,128)(2,1)}, bf16[2,512,320]{1,2,0:T(8,128)(2,1)}, u32[]{:S(2)}, u32[]{:S(2)}) collective-permute-start(bf16[2,512,320]{1,2,0:T(8,128)(2,1)} %pad_maximum_fusion.4), channel_id=1, source_target_pairs={{0,4},{4,8},{8,12},{12,16},{16,20},{20,24},{24,28},{1,5},{5,9},{9,... | collective-permute-start | bytes 1966088 | tf_op jit(solution)/shard_map/ppermute | solution.py:14
  177.3 7.9 %copy-start.7 = (bf16[1024,320]{0,1:T(8,128)(2,1)S(1)}, bf16[1024,320]{0,1:T(8,128)(2,1)}, u32[]{:S(2)}) copy-start(bf16[1024,320]{0,1:T(8,128)(2,1)} %copy-done.6) | copy-start | bytes 1966084
  186.5 9.0 %copy-start.14 = (bf16[1024,320]{0,1:T(8,128)(2,1)S(1)}, bf16[1024,320]{0,1:T(8,128)(2,1)}, u32[]{:S(2)}) copy-start(bf16[1024,320]{0,1:T(8,128)(2,1)} %get-tuple-element.32) | copy-start | bytes 1966084
  195.5 5.9 %copy-start.21 = (bf16[320,1280]{1,0:T(8,128)(2,1)S(1)}, bf16[320,1280]{1,0:T(8,128)(2,1)}, u32[]{:S(2)}) copy-start(bf16[320,1280]{1,0:T(8,128)(2,1)} %param.29) | copy-start | bytes 2457604
  195.5 5.9 %copy-start.24 = (bf16[5,64,512]{2,1,0:T(8,128)(2,1)S(1)}, bf16[5,64,512]{2,1,0:T(8,128)(2,1)}, u32[]{:S(2)}) copy-start(bf16[5,64,512]{2,1,0:T(8,128)(2,1)} %fusion.31) | copy-start | bytes 983044
  204.7 53.5 %all-gather.11.cloned.1.call-start = ((), (), s32[]{:S(2)}) async-start(), calls=%async_computation.8 | async-start | bytes 2580480 | tf_op jit(solution)/shard_map/all_gather | solution.py:141
  205.3 105.9 %all-gather.9.cloned.1.call-start = ((), (), s32[]{:S(2)}) async-start(), calls=%async_computation.7 | async-start | bytes 3276800 | tf_op jit(solution)/shard_map/all_gather | solution.py:138
  253.6 1.9 copy-start.1
  253.6 2.1 copy-start.3
  256.8 84.2 %all-gather.13.cloned.1.call-start = ((), (), s32[]{:S(2)}) async-start(), calls=%async_computation.9 | async-start | bytes 2580480 | tf_op jit(solution)/shard_map/all_gather | solution.py:145
  257.4 114.1 %all-gather.15.cloned.1.call-start = ((), (), s32[]{:S(2)}) async-start(), calls=%async_computation.10 | async-start | bytes 2580480 | tf_op jit(solution)/shard_map/all_gather | solution.py:150
  258.1 176.5 %reduce-scatter.5.cloned.1.call-start = ((), (), s32[]{:S(2)}) async-start(), calls=%async_computation.11 | async-start | bytes 3276800 | tf_op jit(solution)/shard_map/reduce_scatter | solution.py:153
  382.9 109.7 %all-gather.17.cloned.1.call-start = ((), (), s32[]{:S(2)}) async-start(), calls=%async_computation.12 | async-start | bytes 3276800 | tf_op jit(solution)/shard_map/all_gather | solution.py:157
  434.6 2.0 copy-start.2
  434.6 2.1 copy-start.8
  436.6 1.3 copy-start.17
  437.8 133.6 %all-reduce.2.cloned.1.call-start = ((), (), s32[]{:S(2)}) async-start(), calls=%async_computation.13 | async-start | bytes 163840 | tf_op jit(solution)/shard_map/psum | solution.py:214
  437.9 5.7 collective-permute-start
  492.6 8.4 %copy-start.5 = (bf16[1024,1280]{1,0:T(8,128)(2,1)S(1)}, bf16[1024,1280]{1,0:T(8,128)(2,1)}, u32[]{:S(2)}) copy-start(bf16[1024,1280]{1,0:T(8,128)(2,1)} %all-gather.17.cloned.1.call-done) | copy-start | bytes 7864324
  492.6 8.4 %copy-start.22 = (bf16[1280,320]{0,1:T(8,128)(2,1)S(1)}, bf16[1280,320]{0,1:T(8,128)(2,1)}, u32[]{:S(2)}) copy-start(bf16[1280,320]{0,1:T(8,128)(2,1)} %param.34) | copy-start | bytes 2457604
  494.6 29.1 %collective-permute-start.2 = (bf16[512,1280]{1,0:T(8,128)(2,1)S(1)}, bf16[512,1280]{1,0:T(8,128)(2,1)S(1)}, u32[]{:S(2)}, u32[]{:S(2)}) collective-permute-start(bf16[512,1280]{1,0:T(8,128)(2,1)S(1)} %get-tuple-element.10), channel_id=1, source_target_pairs={{0,4},{4,8},{8,12},{12,16},{16,20},{20,24},{24,28},{1,5},{5,9},{9,... | collective-permute-start | bytes 3932168 | tf_op jit(solution)/shard_map/ppermute | solution.py:25
  498.6 29.9 %collective-permute-start.3 = (bf16[512,1280]{1,0:T(8,128)(2,1)S(1)}, bf16[512,1280]{1,0:T(8,128)(2,1)S(1)}, u32[]{:S(2)}, u32[]{:S(2)}) collective-permute-start(bf16[512,1280]{1,0:T(8,128)(2,1)S(1)} %get-tuple-element.11), channel_id=1, source_target_pairs={{4,0},{8,4},{12,8},{16,12},{20,16},{24,20},{28,24},{5,1},{9,5},{13... | collective-permute-start | bytes 3932168 | tf_op jit(solution)/shard_map/ppermute | solution.py:27
  501.0 1.9 copy-start.23
  531.6 1.7 copy-start.10
  532.7 0.7 copy-start.12
  535.1 1.8 copy-start.13
  535.1 1.9 copy-start.11
  535.4 1.1 copy-start.4
  538.2 2.9 copy-start.9
Sparse Core Ops, SparseCore 0:
  103.8 53.9 all-gather.6
  204.8 48.7 reduce-scatter.2
  383.0 51.5 reduce-scatter.4
  438.0 54.6 all-gather.16
Sparse Core Ops, SparseCore 1:
  207.1 25.7 all-gather.10
  256.9 54.3 all-gather.8
  313.0 27.9 all-gather.12
  342.8 28.5 all-gather.14
  542.0 29.3 all-reduce.1
where the time goes:
time: 585 us; the launch traced here: 581 us
  waiting for transfers between devices  378 us (65%)
  matrix products  74.6 us (13%)
  local copies, waits for them, and re-layouts  50.8 us (9%)
  starting transfers between devices  21.7 us (4%)
  blocking collectives  20.6 us (4%)
  other arithmetic  19.7 us (3%)
  between operations  15.9 us (3%)
    all_gather x1, waiting for transfers between devices, per_device(): mlp_in = lax.all_gather(normed, 'mp', axis=0, tiled=True)  53.1 us
    reduce_scatter x1, waiting for transfers between devices, per_device(): lax.psum_scatter(down_terms.astype(jnp.bfloat16), 'mp', scatter_dimension...  51.6 us
    all_gather x1, waiting for transfers between devices, per_device(): layer_in = lax.all_gather(normed, 'mp', axis=0, tiled=True)  51.3 us
    all_gather x1, waiting for transfers between devices, per_device(): states = lax.all_gather(encoded, 'mp', axis=0, tiled=True)  48.4 us
    reduce_scatter x1, waiting for transfers between devices, per_device(): lax.psum_scatter(jnp.dot(heads_out, w_attn_out, preferred_element_type=jn...  45.5 us
    all_gather x1, waiting for transfers between devices, per_device(): lax.all_gather(w_down, 'seq', axis=1, tiled=True)  30.5 us
    psum x1, waiting for transfers between devices, per_device(): lax.psum(jnp.dot(cross_heads, w_cross_out, preferred_element_type=jnp.flo...  29.5 us
    all_gather x1, waiting for transfers between devices, per_device(): lax.all_gather(w_up, 'seq', axis=0, tiled=True)  22.6 us
  transfers between devices with their start and end apart: 15, of which 12 were waited for; matrix products, arithmetic and copies ran while one was open for 7% of the time, Pallas kernels for 0%

commit v1 on v0

--- a/solution.py
+++ b/solution.py
@@ -77,22 +77,42 @@
     earlier = (line[:, None] > line[None, :]).astype(jnp.bfloat16)
     before = jnp.dot(earlier, owner_hot, preferred_element_type=jnp.float32)
     order = jnp.sum(before * owner_hot.astype(jnp.float32), axis=1).astype(jnp.int32)
-    requests = jnp.zeros((seq_count, capacity), jnp.int32).at[owner, order].set(hash_slot)
-    found = jnp.take(
-        hash_table, lax.all_to_all(requests, "seq", split_axis=0, concat_axis=0, tiled=True), axis=0
-    )
-    fetched = lax.all_to_all(found, "seq", split_axis=0, concat_axis=0, tiled=True)
-    hash_rows = fetched[owner, order]
+    target = owner * capacity + order
+    chosen = (target[:, None] == jnp.arange(seq_count * capacity, dtype=jnp.int32)[None, :]).astype(
+        jnp.bfloat16
+    )
+    digits = jnp.stack([hash_slot // 64, hash_slot % 64], axis=0).astype(jnp.bfloat16)
+    asked = jnp.dot(digits, chosen, preferred_element_type=jnp.float32).astype(jnp.int32)
+    requests = (asked[0] * 64 + asked[1]).reshape(seq_count, capacity)
+    wanted = lax.all_to_all(requests, "seq", split_axis=0, concat_axis=0, tiled=True).reshape(-1)
+    picked = (
+        wanted[:, None] == jnp.arange(hash_table.shape[0], dtype=jnp.int32)[None, :]
+    ).astype(jnp.bfloat16)
+    found = jnp.dot(picked, hash_table, preferred_element_type=jnp.float32).astype(jnp.bfloat16)
+    fetched = lax.all_to_all(
+        found.reshape(seq_count, capacity, -1), "seq", split_axis=0, concat_axis=0, tiled=True
+    ).reshape(seq_count * capacity, -1)
+    hash_rows = jnp.dot(chosen, fetched, preferred_element_type=jnp.float32)
     byte_hot = (byte_values[:, None] == jnp.arange(256, dtype=jnp.int32)[None, :]).astype(
         jnp.bfloat16
     )
     byte_rows = jnp.dot(byte_hot, byte_table, preferred_element_type=jnp.float32)
-    embed = (byte_rows + hash_rows.astype(jnp.float32)).astype(jnp.bfloat16)
-    residual = lax.all_to_all(embed, "mp", split_axis=0, concat_axis=1, tiled=True).astype(
-        jnp.float32
-    )
-    normed = rms_scale(residual, norm_gains[0]).astype(jnp.bfloat16)
-    layer_in = lax.all_gather(normed, "mp", axis=0, tiled=True)
+    embed = (byte_rows + hash_rows).astype(jnp.bfloat16)
+    full_gate = lax.all_gather(w_gate, "seq", axis=0, tiled=True)
+    full_up = lax.all_gather(w_up, "seq", axis=0, tiled=True)
+    full_down = lax.all_gather(w_down, "seq", axis=1, tiled=True)
+    embed, full_gate, full_up, full_down = lax.optimization_barrier(
+        (embed, full_gate, full_up, full_down)
+    )
+    embed_parts = lax.all_gather(embed, "mp", axis=0, tiled=False)
+    embed_full = jnp.concatenate(
+        [embed_parts[i] for i in range(embed_parts.shape[0])], axis=1
+    )
+    share = length // lax.axis_size("mp")
+    residual = lax.dynamic_slice_in_dim(
+        embed_full, lax.axis_index("mp") * share, share, axis=0
+    ).astype(jnp.float32)
+    layer_in = rms_scale(embed_full.astype(jnp.float32), norm_gains[0]).astype(jnp.bfloat16)
     queries = jnp.dot(layer_in, w_query, preferred_element_type=jnp.float32).astype(jnp.bfloat16)
     keys = jnp.dot(layer_in, w_key, preferred_element_type=jnp.float32).astype(jnp.bfloat16)
     values = jnp.dot(layer_in, w_value, preferred_element_type=jnp.float32).astype(jnp.bfloat16)
@@ -138,16 +158,16 @@
     mlp_in = lax.all_gather(normed, "mp", axis=0, tiled=True)
     gate = jnp.dot(
         mlp_in,
-        lax.all_gather(w_gate, "seq", axis=0, tiled=True),
+        full_gate,
         preferred_element_type=jnp.float32,
     )
     lifted = jnp.dot(
-        mlp_in, lax.all_gather(w_up, "seq", axis=0, tiled=True), preferred_element_type=jnp.float32
+        mlp_in, full_up, preferred_element_type=jnp.float32
     )
     hidden = (jax.nn.silu(gate) * lifted).astype(jnp.bfloat16)
     down_terms = jnp.dot(
         hidden,
-        lax.all_gather(w_down, "seq", axis=1, tiled=True),
+        full_down,
         preferred_element_type=jnp.float32,
     )
     residual = residual + lax.psum_scatter(
@@ -211,10 +231,15 @@
         .reshape(patch_count, local_width)
     )
     pooled, cross_heads = (pooled, cross_heads)
-    mixed_patches = lax.psum(
-        jnp.dot(cross_heads, w_cross_out, preferred_element_type=jnp.float32).astype(jnp.bfloat16),
-        "mp",
-    ).astype(jnp.float32)
+    own_share = jnp.dot(cross_heads, w_cross_out, preferred_element_type=jnp.float32).astype(
+        jnp.bfloat16
+    )
+    mp_count = lax.axis_size("mp")
+    mixed_patches = own_share.astype(jnp.float32)
+    for step in range(1, mp_count):
+        mixed_patches = mixed_patches + lax.ppermute(
+            own_share, "mp", [(i, (i + step) % mp_count) for i in range(mp_count)]
+        ).astype(jnp.float32)
     patch_hidden = (pooled + mixed_patches).astype(jnp.bfloat16)
     return jnp.dot(patch_hidden, w_global, preferred_element_type=jnp.float32).astype(jnp.bfloat16)
 

time: 585 us -> 527 us (0.901)
  local copies, waits for them, and re-layouts: 50.8 us -> 11.4 us
  waiting for transfers between devices: 378 us -> 345 us
  blocking collectives: 20.6 us -> 32.3 us
  starting transfers between devices: 21.7 us -> 14.6 us
  matrix products: 74.6 us -> 81.6 us
    psum x1 -> x0, waiting for transfers between devices: 29.5 us -> none  [per_device(): lax.psum(jnp.dot(cross_heads, w_cross_out, preferred_element_type=jnp.flo...]
    gather x4 -> x0, local copies, waits for them, and re-layouts: 28.2 us -> none  [the longest x2 14.6 us: per_device(): hash_rows = fetched[owner, order]]
    all_to_all x2 -> x0, waiting for transfers between devices: 16.8 us -> none  [the longest x1 16.8 us: per_device(): lax.all_to_all(embed, 'mp', split_axis=0, concat_axis=1, tiled=True)]
    all_to_all x1 -> x2, blocking collectives: 20.6 us -> 32.3 us  [the longest x1 24.6 us: per_device(): lax.all_to_all(found.reshape(seq_count, capacity, -1), 'seq', split_axis=...]
    dot_general x2 -> x5, matrix products: 18.6 us -> 28 us  [the longest x1 10.9 us: per_device(): down_terms = jnp.dot(hidden, full_down, preferred_element_type=jnp.float32)]
    all_to_all x2 -> x0, starting transfers between devices: 9.16 us -> none  [the longest x1 4.59 us: per_device(): lax.all_to_all(embed, 'mp', split_axis=0, concat_axis=1, tiled=True)]
    unnamed x53 -> x51, local copies, waits for them, and re-layouts: 11.7 us -> 3.74 us
    ppermute x0 -> x3, waiting for transfers between devices: none -> 6.51 us  [per_device(): lax.ppermute(own_share, 'mp', [(i, (i + step) % mp_count) for i in range(...]
where the time goes in v1:
time: 527 us; the launch traced here: 518 us
  waiting for transfers between devices  345 us (65%)
  matrix products  81.6 us (15%)
  blocking collectives  32.3 us (6%)
  other arithmetic  18.2 us (3%)
  between operations  14.9 us (3%)
  starting transfers between devices  14.6 us (3%)
  local copies, waits for them, and re-layouts  11.4 us (2%)
    all_gather x1, waiting for transfers between devices, per_device(): mlp_in = lax.all_gather(normed, 'mp', axis=0, tiled=True)  55 us
    all_gather x1, waiting for transfers between devices, per_device(): embed_parts = lax.all_gather(embed, 'mp', axis=0, tiled=False)  52.5 us
    reduce_scatter x1, waiting for transfers between devices, per_device(): lax.psum_scatter(down_terms.astype(jnp.bfloat16), 'mp', scatter_dimension...  50 us
    reduce_scatter x1, waiting for transfers between devices, per_device(): lax.psum_scatter(jnp.dot(heads_out, w_attn_out, preferred_element_type=jn...  49.3 us
    all_gather x1, waiting for transfers between devices, per_device(): states = lax.all_gather(encoded, 'mp', axis=0, tiled=True)  48.7 us
    all_gather x1, waiting for transfers between devices, per_device(): full_down = lax.all_gather(w_down, 'seq', axis=1, tiled=True)  30.7 us
    all_to_all x1, blocking collectives, per_device(): lax.all_to_all(found.reshape(seq_count, capacity, -1), 'seq', split_axis=...  24.6 us
    all_gather x1, waiting for transfers between devices, per_device(): full_up = lax.all_gather(w_up, 'seq', axis=0, tiled=True)  23.5 us
  transfers between devices with their start and end apart: 15, of which 12 were waited for; matrix products, arithmetic and copies ran while one was open for 7% of the time, Pallas kernels for 0%

profile of v1, /device:TPU:3, one launch (start us, length us, event | category | flops | bytes accessed | tf_op | source)
XLA Modules:
  0.0 517.9 jit_solution(4954972619081522777)
XLA Ops:
  8.8 1.2 fusion.46
  11.5 1.6 fusion.40
  13.1 7.7 %all_to_all.11 = s32[8,1,256]{2,1,0:T(1,128)S(1)} all-to-all(s32[8,1,256]{2,1,0:T(1,128)S(1)} %bitcast.88), channel_id=1, replica_groups=mesh['seq'=8,'mp'=4] {'seq'}, dimensions={0} | all-to-all | bytes 16384 | tf_op jit(solution)/shard_map/all_to_all | solution.py:87
  20.7 6.4 %fusion.33 = bf16[2048,320]{0,1:T(8,128)(2,1)S(1)} fusion(bf16[4096,320]{0,1:T(8,128)(2,1)S(1)} %copy-done, s32[2048]{0:T(1024)S(1)} %bitcast.90), kind=kOutput, calls=%fused_computation.45 | convolution fusion | flops 5377753088 | bytes 3940352 | tf_op jit(solution)/shard_map/dot_general | solution.py:91
  27.2 24.6 %all_to_all.12 = bf16[8,256,320]{1,2,0:T(8,128)(2,1)S(1)} all-to-all(bf16[8,256,320]{1,2,0:T(8,128)(2,1)S(1)} %bitcast.75), channel_id=1, replica_groups=mesh['seq'=8,'mp'=4] {'seq'}, dimensions={0} | all-to-all | bytes 2621440 | tf_op jit(solution)/shard_map/all_to_all | solution.py:92
  52.0 1.9 fusion.5
  53.9 1.3 fusion.41
  55.2 23.5 %all-gather.10.cloned.1.call-done = bf16[1280,896]{1,0:T(8,128)(2,1)} async-done(((bf16[160,896]{1,0:T(8,128)(2,1)}), bf16[1280,896]{1,0:T(8,128)(2,1)}) %all-gather.10.cloned.1.call-update) | async-done | bytes 2293776 | tf_op jit(solution)/shard_map/all_gather | solution.py:102
  78.7 30.7 %all-gather.12.cloned.1.call-done = bf16[896,1280]{0,1:T(8,128)(2,1)} async-done(((bf16[896,160]{0,1:T(8,128)(2,1)}), bf16[896,1280]{0,1:T(8,128)(2,1)}) %all-gather.12.cloned.1.call-update) | async-done | bytes 2293776 | tf_op jit(solution)/shard_map/all_gather | solution.py:103
  109.9 1.3 and_and_fusion
  111.3 1.4 and_and_fusion.1
  112.7 52.5 %all-gather.18.cloned.1.call-done = bf16[4096,320]{0,1:T(8,128)(2,1)} async-done(((bf16[1024,320]{0,1:T(8,128)(2,1)}), bf16[4096,320]{0,1:T(8,128)(2,1)}) %all-gather.18.cloned.1.call-update) | async-done | bytes 2621456 | tf_op jit(solution)/shard_map/all_gather | solution.py:107
  165.2 1.9 fusion.75
  168.3 1.1 convolution_convert_fusion.8
  174.9 3.6 collective-permute-start.1
  178.5 9.0 %fusion.79 = (f32[5,512]{1,0:T(8,128)S(1)}, f32[5,512,1024]{2,1,0:T(8,128)}) fusion(pred[512,1024]{1,0:T(8,128)(4,1)} %and_and_fusion, bf16[512,5,64]{0,2,1:T(8,128)(2,1)} %bitcast.87, bf16[1024,5,64]{0,2,1:T(8,128)(2,1)} %bitcast.80), kind=kOutput, calls=%fused_computation.149 | convolution fusion | flops 346031104 | bytes 12003328 | tf_op jit(solution)/shard_map/sub | solution.py:41
  187.5 6.5 %fusion.42 = bf16[5,64,512]{2,1,0:T(8,128)(2,1)} fusion(bf16[1024,5,64]{0,2,1:T(8,128)(2,1)S(1)} %bitcast.78, f32[5,512,1024]{2,1,0:T(8,128)} %get-tuple-element.35, f32[5,512]{1,0:T(8,128)S(1)} %get-tuple-element.34), kind=kOutput, calls=%fused_computation.75 | convolution fusion | flops 340951040 | bytes 11479040 | tf_op jit(solution)/shard_map/hqk,khd->qhd/dot_general | solution.py:146
  195.2 1.2 pad_maximum_fusion.3
  196.4 9.1 %fusion.80 = (f32[5,512]{1,0:T(8,128)S(1)}, f32[5,512,1024]{2,1,0:T(8,128)}) fusion(pred[512,1024]{1,0:T(8,128)(4,1)} %and_and_fusion.1, bf16[512,5,64]{0,2,1:T(8,128)(2,1)} %bitcast.86, bf16[1024,5,64]{0,2,1:T(8,128)(2,1)} %bitcast.85), kind=kOutput, calls=%fused_computation.150 | convolution fusion | flops 346031104 | bytes 12003328 | tf_op jit(solution)/shard_map/sub | solution.py:41
  205.5 5.8 %fusion.43 = bf16[5,64,512]{2,1,0:T(8,128)(2,1)S(1)} fusion(bf16[1024,5,64]{0,2,1:T(8,128)(2,1)S(1)} %bitcast.84, f32[5,512,1024]{2,1,0:T(8,128)} %get-tuple-element.37, f32[5,512]{1,0:T(8,128)S(1)} %get-tuple-element.36), kind=kOutput, calls=%fused_computation.76 | convolution fusion | flops 340951040 | bytes 11479040 | tf_op jit(solution)/shard_map/hqk,khd->qhd/dot_general | solution.py:146
  211.3 3.1 convolution_convert_fusion.1
  214.7 49.3 %reduce-scatter.3.cloned.1.call-done = bf16[256,1280]{0,1:T(8,128)(2,1)} async-done(((bf16[1024,1280]{0,1:T(8,128)(2,1)}), bf16[256,1280]{0,1:T(8,128)(2,1)}) %reduce-scatter.3.cloned.1.call-update) | async-done | bytes 655376 | tf_op jit(solution)/shard_map/reduce_scatter | solution.py:151
  263.9 1.4 multiply_reduce_fusion.1
  265.3 2.2 multiply_convert_fusion.2
  267.6 55.0 %all-gather.14.cloned.1.call-done = bf16[1024,1280]{0,1:T(8,128)(2,1)} async-done(((bf16[256,1280]{0,1:T(8,128)(2,1)}), bf16[1024,1280]{0,1:T(8,128)(2,1)}) %all-gather.14.cloned.1.call-update) | async-done | bytes 2621456 | tf_op jit(solution)/shard_map/all_gather | solution.py:158
  322.6 7.3 %fusion.82 = f32[1024,896]{1,0:T(8,128)} fusion(bf16[1024,1280]{0,1:T(8,128)(2,1)} %all-gather.14.cloned.1.call-done, bf16[1280,896]{1,0:T(8,128)(2,1)} %all-gather.8.cloned.1.call-done), kind=kOutput, calls=%fused_computation.152 | convolution fusion | flops 2348810240 | bytes 8585216 | tf_op jit(solution)/shard_map/dot_general | solution.py:159
  329.9 10.9 %convolution_convert_fusion = bf16[1024,1280]{0,1:T(8,128)(2,1)} fusion(bf16[896,1280]{0,1:T(8,128)(2,1)} %all-gather.12.cloned.1.call-done, f32[1024,896]{1,0:T(8,128)} %fusion.82, bf16[1024,1280]{0,1:T(8,128)(2,1)S(1)} %copy-done.17, bf16[1280,896]{1,0:T(8,128)(2,1)} %all-gather.10.cloned.1.call-done), kind=kOutput, calls=%fused_computation.42 | convolution fusion | flops 4704436224 | bytes 13500416 | tf_op jit(solution)/shard_map/dot_general | solution.py:168
  340.9 50.0 %reduce-scatter.5.cloned.1.call-done = bf16[256,1280]{0,1:T(8,128)(2,1)} async-done(((bf16[1024,1280]{0,1:T(8,128)(2,1)}), bf16[256,1280]{0,1:T(8,128)(2,1)}) %reduce-scatter.5.cloned.1.call-update) | async-done | bytes 655376 | tf_op jit(solution)/shard_map/reduce_scatter | solution.py:173
  390.9 1.6 multiply_reduce_fusion
  392.5 2.4 multiply_convert_fusion.1
  395.0 2.8 collective-permute-start
  397.9 2.9 collective-permute-done
  401.4 48.7 %all-gather.16.cloned.1.call-done = bf16[1024,1280]{0,1:T(8,128)(2,1)} async-done(((bf16[256,1280]{0,1:T(8,128)(2,1)}), bf16[1024,1280]{0,1:T(8,128)(2,1)}) %all-gather.16.cloned.1.call-update) | async-done | bytes 2621456 | tf_op jit(solution)/shard_map/all_gather | solution.py:177
  450.1 2.0 fusion.74
  452.1 3.4 collective-permute-start.2
  455.9 2.1 collective-permute-start.3
  458.2 1.9 convolution_convert_fusion.5
  460.0 1.9 convolution_convert_fusion.3
  461.9 19.1 %collective-permute-done.2 = bf16[512,1280]{0,1:T(8,128)(2,1)S(1)} collective-permute-done((bf16[512,1280]{0,1:T(8,128)(2,1)S(1)}, bf16[512,1280]{0,1:T(8,128)(2,1)S(1)}, u32[]{:S(2)}, u32[]{:S(2)}) %collective-permute-start.2) | collective-permute-done | bytes 1310752 | tf_op jit(solution)/shard_map/ppermute | solution.py:25
  481.2 4.6 collective-permute-done.3
  489.0 1.6 fusion.37
  491.7 1.4 pad_maximum_fusion.2
  495.0 1.2 pad_maximum_fusion.1
  496.2 2.8 fusion.44
  499.9 1.4 collective-permute-start.4
  501.3 3.0 collective-permute-done.6
  504.2 3.5 collective-permute-done.5
  507.8 3.0 convolution_convert_fusion.10
  (113 shorter events, 20.1 us)
Async XLA Ops:
  6.5 14.2 %copy-start = (bf16[4096,320]{0,1:T(8,128)(2,1)S(1)}, bf16[4096,320]{0,1:T(8,128)(2,1)}, u32[]{:S(2)}) copy-start(bf16[4096,320]{0,1:T(8,128)(2,1)} %param.24) | copy-start | bytes 7864324
  6.5 48.7 %all-gather.8.cloned.1.call-start = ((), (), s32[]{:S(2)}) async-start(), calls=%async_computation.4 | async-start | bytes 2580480 | tf_op jit(solution)/shard_map/all_gather | solution.py:101
  7.3 71.5 %all-gather.10.cloned.1.call-start = ((), (), s32[]{:S(2)}) async-start(), calls=%async_computation.5 | async-start | bytes 2580480 | tf_op jit(solution)/shard_map/all_gather | solution.py:102
  8.0 101.4 %all-gather.12.cloned.1.call-start = ((), (), s32[]{:S(2)}) async-start(), calls=%async_computation.6 | async-start | bytes 2580480 | tf_op jit(solution)/shard_map/all_gather | solution.py:103
  8.7 156.4 %all-gather.18.cloned.1.call-start = ((), (), s32[]{:S(2)}) async-start(), calls=%async_computation.11 | async-start | bytes 3276800 | tf_op jit(solution)/shard_map/all_gather | solution.py:107
  52.0 1.9 copy-start.13
  52.0 1.9 copy-start.15
  53.9 56.0 %copy-start.14 = (f32[3,1280]{1,0:T(4,128)S(1)}, f32[3,1280]{1,0:T(4,128)}, u32[]{:S(2)}) copy-start(f32[3,1280]{1,0:T(4,128)} %param.25) | copy-start | bytes 46084
  109.4 154.5 %reduce-scatter.3.cloned.1.call-start = ((), (), s32[]{:S(2)}) async-start(), calls=%async_computation.7 | async-start | bytes 3276800 | tf_op jit(solution)/shard_map/reduce_scatter | solution.py:151
  167.1 1.1 copy-start.18
  168.0 97.3 %copy-start.3 = (bf16[1024,1280]{0,1:T(8,128)(2,1)}, bf16[1024,1280]{0,1:T(8,128)(2,1)S(1)}, u32[]{:S(2)}) copy-start(bf16[1024,1280]{0,1:T(8,128)(2,1)S(1)} %get-tuple-element.17) | copy-start | bytes 7864324
  168.3 1.8 copy-start.19
  170.0 2.0 copy-start.20
  173.1 0.9 copy-start.6
  174.9 19.2 %collective-permute-start.1 = (bf16[2,512,320]{1,2,0:T(8,128)(2,1)}, bf16[2,512,320]{1,2,0:T(8,128)(2,1)}, u32[]{:S(2)}, u32[]{:S(2)}) collective-permute-start(bf16[2,512,320]{1,2,0:T(8,128)(2,1)} %pad_maximum_fusion.5), channel_id=1, source_target_pairs={{0,4},{4,8},{8,12},{12,16},{16,20},{20,24},{24,28},{1,5},{5,9},{9,... | collective-permute-start | bytes 1966088 | tf_op jit(solution)/shard_map/ppermute | solution.py:14
  187.5 7.7 %copy-start.7 = (bf16[1024,320]{0,1:T(8,128)(2,1)S(1)}, bf16[1024,320]{0,1:T(8,128)(2,1)}, u32[]{:S(2)}) copy-start(bf16[1024,320]{0,1:T(8,128)(2,1)} %copy-done.6) | copy-start | bytes 1966084
  196.4 9.1 %copy-start.12 = (bf16[1024,320]{0,1:T(8,128)(2,1)S(1)}, bf16[1024,320]{0,1:T(8,128)(2,1)}, u32[]{:S(2)}) copy-start(bf16[1024,320]{0,1:T(8,128)(2,1)} %get-tuple-element.43) | copy-start | bytes 1966084
  205.5 5.9 %copy-start.21 = (bf16[320,1280]{1,0:T(8,128)(2,1)S(1)}, bf16[320,1280]{1,0:T(8,128)(2,1)}, u32[]{:S(2)}) copy-start(bf16[320,1280]{1,0:T(8,128)(2,1)} %param.29) | copy-start | bytes 2457604
  205.5 5.9 %copy-start.24 = (bf16[5,64,512]{2,1,0:T(8,128)(2,1)S(1)}, bf16[5,64,512]{2,1,0:T(8,128)(2,1)}, u32[]{:S(2)}) copy-start(bf16[5,64,512]{2,1,0:T(8,128)(2,1)} %fusion.42) | copy-start | bytes 983044
  214.4 108.2 %all-gather.14.cloned.1.call-start = ((), (), s32[]{:S(2)}) async-start(), calls=%async_computation.8 | async-start | bytes 3276800 | tf_op jit(solution)/shard_map/all_gather | solution.py:158
  267.5 123.4 %reduce-scatter.5.cloned.1.call-start = ((), (), s32[]{:S(2)}) async-start(), calls=%async_computation.9 | async-start | bytes 3276800 | tf_op jit(solution)/shard_map/reduce_scatter | solution.py:173
  322.6 7.3 %copy-start.17 = (bf16[1024,1280]{0,1:T(8,128)(2,1)S(1)}, bf16[1024,1280]{0,1:T(8,128)(2,1)}, u32[]{:S(2)}) copy-start(bf16[1024,1280]{0,1:T(8,128)(2,1)} %all-gather.14.cloned.1.call-done) | copy-start | bytes 7864324
  340.8 50.1 %copy-start.2 = (bf16[256,1280]{0,1:T(8,128)(2,1)S(1)}, bf16[256,1280]{0,1:T(8,128)(2,1)}, u32[]{:S(2)}) copy-start(bf16[256,1280]{0,1:T(8,128)(2,1)} %reduce-scatter.3.cloned.1.call-done) | copy-start | bytes 1966084
  340.8 54.2 %copy-start.16 = (s32[32]{0:T(128)S(1)}, s32[32]{0:T(128)}, u32[]{:S(2)}) copy-start(s32[32]{0:T(128)} %param.22) | copy-start | bytes 388
  340.8 109.2 %all-gather.16.cloned.1.call-start = ((), (), s32[]{:S(2)}) async-start(), calls=%async_computation.10 | async-start | bytes 3276800 | tf_op jit(solution)/shard_map/all_gather | solution.py:177
  395.0 5.7 %collective-permute-start = (s32[1]{0:T(128)S(1)}, s32[1]{0:T(128)}, u32[]{:S(2)}, u32[]{:S(2)}) collective-permute-start(s32[1]{0:T(128)S(1)} %bitcast.94), channel_id=1, source_target_pairs={{4,0},{8,4},{12,8},{16,12},{20,16},{24,20},{28,24},{5,1},{9,5},{13... | collective-permute-start | bytes 20 | tf_op jit(solution)/shard_map/ppermute | solution.py:14
  450.1 8.1 %copy-start.5 = (bf16[1024,1280]{0,1:T(8,128)(2,1)S(1)}, bf16[1024,1280]{0,1:T(8,128)(2,1)}, u32[]{:S(2)}) copy-start(bf16[1024,1280]{0,1:T(8,128)(2,1)} %all-gather.16.cloned.1.call-done) | copy-start | bytes 7864324
  450.1 8.1 %copy-start.22 = (bf16[1280,320]{0,1:T(8,128)(2,1)S(1)}, bf16[1280,320]{0,1:T(8,128)(2,1)}, u32[]{:S(2)}) copy-start(bf16[1280,320]{0,1:T(8,128)(2,1)} %param.35) | copy-start | bytes 2457604
  452.1 28.9 %collective-permute-start.2 = (bf16[512,1280]{0,1:T(8,128)(2,1)S(1)}, bf16[512,1280]{0,1:T(8,128)(2,1)S(1)}, u32[]{:S(2)}, u32[]{:S(2)}) collective-permute-start(bf16[512,1280]{0,1:T(8,128)(2,1)S(1)} %get-tuple-element.18), channel_id=1, source_target_pairs={{0,4},{4,8},{8,12},{12,16},{16,20},{20,24},{24,28},{1,5},{5,9},{9,... | collective-permute-start | bytes 3932168 | tf_op jit(solution)/shard_map/ppermute | solution.py:25
  455.9 29.9 %collective-permute-start.3 = (bf16[512,1280]{0,1:T(8,128)(2,1)S(1)}, bf16[512,1280]{0,1:T(8,128)(2,1)S(1)}, u32[]{:S(2)}, u32[]{:S(2)}) collective-permute-start(bf16[512,1280]{0,1:T(8,128)(2,1)S(1)} %get-tuple-element.19), channel_id=1, source_target_pairs={{4,0},{8,4},{12,8},{16,12},{20,16},{24,20},{28,24},{5,1},{9,5},{13... | collective-permute-start | bytes 3932168 | tf_op jit(solution)/shard_map/ppermute | solution.py:27
  458.1 1.9 copy-start.23
  489.0 2.3 copy-start.9
  490.6 0.7 copy-start.11
  493.2 1.8 copy-start.10
  493.6 1.1 copy-start.4
  496.2 3.0 copy-start.8
  496.2 14.6 %copy-start.1 = (bf16[4096,320]{0,1:T(8,128)(2,1)S(1)}, bf16[4096,320]{0,1:T(8,128)(2,1)}, u32[]{:S(2)}) copy-start(bf16[4096,320]{0,1:T(8,128)(2,1)} %param.24) | copy-start | bytes 7864324
  499.4 4.8 collective-permute-start.6
  499.7 8.1 %collective-permute-start.5 = (bf16[32,1280]{1,0:T(8,128)(2,1)S(1)}, bf16[32,1280]{1,0:T(8,128)(2,1)S(1)}, u32[]{:S(2)}, u32[]{:S(2)}) collective-permute-start(bf16[32,1280]{1,0:T(8,128)(2,1)S(1)} %convolution_convert_fusion.2), channel_id=1, source_target_pairs={{0,2},{1,3},{2,0},{3,1},{4,6},{5,7},{6,4},{7,5},{8,10},{9,11},{10,... | collective-permute-start | bytes 245768 | tf_op jit(solution)/shard_map/ppermute | solution.py:240
  499.9 7.9 %collective-permute-start.4 = (bf16[32,1280]{1,0:T(8,128)(2,1)S(1)}, bf16[32,1280]{1,0:T(8,128)(2,1)S(1)}, u32[]{:S(2)}, u32[]{:S(2)}) collective-permute-start(bf16[32,1280]{1,0:T(8,128)(2,1)S(1)} %convolution_convert_fusion.2), channel_id=1, source_target_pairs={{0,1},{1,2},{2,3},{3,0},{4,5},{5,6},{6,7},{7,4},{8,9},{9,10},{10,1... | collective-permute-start | bytes 245768 | tf_op jit(solution)/shard_map/ppermute | solution.py:240
Sparse Core Ops, SparseCore 0:
  9.2 39.2 all-gather.7
  50.4 28.2 all-gather.9
  80.6 28.7 all-gather.11
  110.8 54.3 all-gather.17
  214.6 49.3 reduce-scatter.2
  267.6 54.9 all-gather.13
  340.9 49.9 reduce-scatter.4
  395.1 54.9 all-gather.15

commit v2 on v1

--- a/solution.py
+++ b/solution.py
@@ -40,6 +40,29 @@
     highest = jnp.max(scores, axis=-1, keepdims=True)
     raised = jnp.exp(scores - highest)
     return raised / jnp.sum(raised, axis=-1, keepdims=True)
+
+
+def spread_weights(own):
+    count = lax.axis_size("seq")
+    position = lax.axis_index("seq")
+    pairs = count // 2
+    near = [own]
+    for step in range(1, pairs):
+        near.append(lax.ppermute(own, "seq", [(i, (i + 2 * step) % count) for i in range(count)]))
+    near = jnp.stack(near)
+    far = lax.ppermute(near, "seq", [(i, i ^ 1) for i in range(count)])
+    even = position % 2 == 0
+    both = jnp.stack([jnp.where(even, near, far), jnp.where(even, far, near)], axis=1)
+    ordered = jnp.stack(
+        [
+            lax.dynamic_index_in_dim(both, (position // 2 - i) % pairs, keepdims=False)
+            for i in range(pairs)
+        ]
+    )
+    return [
+        ordered[:, :, part].reshape(count * own.shape[1], own.shape[2])
+        for part in range(own.shape[0])
+    ]
 
 
 def per_device(
@@ -98,21 +121,25 @@
     )
     byte_rows = jnp.dot(byte_hot, byte_table, preferred_element_type=jnp.float32)
     embed = (byte_rows + hash_rows).astype(jnp.bfloat16)
-    full_gate = lax.all_gather(w_gate, "seq", axis=0, tiled=True)
-    full_up = lax.all_gather(w_up, "seq", axis=0, tiled=True)
-    full_down = lax.all_gather(w_down, "seq", axis=1, tiled=True)
-    embed, full_gate, full_up, full_down = lax.optimization_barrier(
-        (embed, full_gate, full_up, full_down)
-    )
+    packed = jnp.stack([w_gate, w_up, w_down.T])
+    embed, packed = lax.optimization_barrier((embed, packed))
+    full_gate, full_up, full_down = spread_weights(packed)
     embed_parts = lax.all_gather(embed, "mp", axis=0, tiled=False)
     embed_full = jnp.concatenate(
         [embed_parts[i] for i in range(embed_parts.shape[0])], axis=1
     )
-    share = length // lax.axis_size("mp")
-    residual = lax.dynamic_slice_in_dim(
-        embed_full, lax.axis_index("mp") * share, share, axis=0
-    ).astype(jnp.float32)
+    mp_count = lax.axis_size("mp")
+    share = WINDOW // mp_count
+    residuals = [
+        lax.dynamic_slice_in_dim(
+            embed_full, block * WINDOW + lax.axis_index("mp") * share, share, axis=0
+        ).astype(jnp.float32)
+        for block in range(length // WINDOW)
+    ]
     layer_in = rms_scale(embed_full.astype(jnp.float32), norm_gains[0]).astype(jnp.bfloat16)
+    layer_in, full_gate, full_up, full_down = lax.optimization_barrier(
+        (layer_in, full_gate, full_up, full_down)
+    )
     queries = jnp.dot(layer_in, w_query, preferred_element_type=jnp.float32).astype(jnp.bfloat16)
     keys = jnp.dot(layer_in, w_key, preferred_element_type=jnp.float32).astype(jnp.bfloat16)
     values = jnp.dot(layer_in, w_value, preferred_element_type=jnp.float32).astype(jnp.bfloat16)
@@ -121,7 +148,6 @@
     key_span = jnp.concatenate([earlier_pair[0], keys], axis=0)
     value_span = jnp.concatenate([earlier_pair[1], values], axis=0)
     first = position * length
-    outputs = []
     for block in range(length // WINDOW):
         query_block = queries[block * WINDOW : (block + 1) * WINDOW].reshape(
             WINDOW, local_heads, HD
@@ -146,40 +172,45 @@
         mixed_block = jnp.einsum(
             "hqk,khd->qhd", weights, value_block, preferred_element_type=jnp.float32
         ).astype(jnp.bfloat16)
-        outputs.append(mixed_block.reshape(WINDOW, local_width))
-    heads_out = jnp.concatenate(outputs, axis=0)
-    residual = residual + lax.psum_scatter(
-        jnp.dot(heads_out, w_attn_out, preferred_element_type=jnp.float32).astype(jnp.bfloat16),
-        "mp",
-        scatter_dimension=0,
-        tiled=True,
-    ).astype(jnp.float32)
-    normed = rms_scale(residual, norm_gains[1]).astype(jnp.bfloat16)
-    mlp_in = lax.all_gather(normed, "mp", axis=0, tiled=True)
-    gate = jnp.dot(
-        mlp_in,
-        full_gate,
-        preferred_element_type=jnp.float32,
-    )
-    lifted = jnp.dot(
-        mlp_in, full_up, preferred_element_type=jnp.float32
-    )
-    hidden = (jax.nn.silu(gate) * lifted).astype(jnp.bfloat16)
-    down_terms = jnp.dot(
-        hidden,
-        full_down,
-        preferred_element_type=jnp.float32,
-    )
-    residual = residual + lax.psum_scatter(
-        down_terms.astype(jnp.bfloat16), "mp", scatter_dimension=0, tiled=True
-    ).astype(jnp.float32)
-    encoded = rms_scale(residual, norm_gains[2]).astype(jnp.bfloat16)
-    states = lax.all_gather(encoded, "mp", axis=0, tiled=True)
-    cross_keys = jnp.dot(states, w_cross_key, preferred_element_type=jnp.float32).astype(
-        jnp.bfloat16
-    )
-    cross_values = jnp.dot(states, w_cross_value, preferred_element_type=jnp.float32).astype(
-        jnp.bfloat16
+        heads_out = mixed_block.reshape(WINDOW, local_width)
+        attn_terms = jnp.dot(heads_out, w_attn_out, preferred_element_type=jnp.float32)
+        residuals[block] = residuals[block] + lax.psum_scatter(
+            attn_terms.astype(jnp.bfloat16), "mp", scatter_dimension=0, tiled=True
+        ).astype(jnp.float32)
+    gathered = []
+    for block, residual in enumerate(residuals):
+        if block > 0:
+            residual, normed = lax.optimization_barrier((residual, normed))
+            residuals[block] = residual
+        normed = rms_scale(residual, norm_gains[1]).astype(jnp.bfloat16)
+        gathered.append(lax.all_gather(normed, "mp", axis=0, tiled=True))
+    encoded_blocks = []
+    for block, (residual, mlp_in) in enumerate(zip(residuals, gathered)):
+        gate = jnp.dot(mlp_in, full_gate, preferred_element_type=jnp.float32)
+        lifted = jnp.dot(mlp_in, full_up, preferred_element_type=jnp.float32)
+        hidden = (jax.nn.silu(gate) * lifted).astype(jnp.bfloat16)
+        down_terms = lax.dot_general(
+            hidden, full_down, (((1,), (1,)), ((), ())), preferred_element_type=jnp.float32
+        )
+        residual = residual + lax.psum_scatter(
+            down_terms.astype(jnp.bfloat16), "mp", scatter_dimension=0, tiled=True
+        ).astype(jnp.float32)
+        if block > 0:
+            residual, encoded_blocks[-1] = lax.optimization_barrier((residual, encoded_blocks[-1]))
+        encoded_blocks.append(rms_scale(residual, norm_gains[2]).astype(jnp.bfloat16))
+    state_blocks = [lax.all_gather(block, "mp", axis=0, tiled=True) for block in encoded_blocks]
+    states = jnp.concatenate(state_blocks, axis=0)
+    cross_keys = jnp.concatenate(
+        [
+            jnp.dot(block, w_cross_key, preferred_element_type=jnp.float32).astype(jnp.bfloat16)
+            for block in state_blocks
+        ]
+    )
+    cross_values = jnp.concatenate(
+        [
+            jnp.dot(block, w_cross_value, preferred_element_type=jnp.float32).astype(jnp.bfloat16)
+            for block in state_blocks
+        ]
     )
     following = passed_along(patch_start[:1], "seq", -1)
     last_end = jnp.where(position == seq_count - 1, seq_count * length, following[0])
@@ -234,7 +265,6 @@
     own_share = jnp.dot(cross_heads, w_cross_out, preferred_element_type=jnp.float32).astype(
         jnp.bfloat16
     )
-    mp_count = lax.axis_size("mp")
     mixed_patches = own_share.astype(jnp.float32)
     for step in range(1, mp_count):
         mixed_patches = mixed_patches + lax.ppermute(

time: 527 us -> 491 us (0.932)
  waiting for transfers between devices: 345 us -> 302 us
  blocking collectives: 32.3 us -> 7.56 us
  matrix products: 81.6 us -> 91 us
  starting transfers between devices: 14.6 us -> 23.8 us
  other arithmetic: 18.2 us -> 25.7 us
    unnamed x8 -> x13, waiting for transfers between devices: 2.17 us -> 110 us
    reduce_scatter x2 -> x0, waiting for transfers between devices: 99.3 us -> none  [the longest x1 50 us: per_device(): lax.psum_scatter(down_terms.astype(jnp.bfloat16), 'mp', scatter_dimension...]
    all_gather x5 -> x4, waiting for transfers between devices: 158 us -> 104 us  [the longest x2 55.3 us: per_device(): lax.all_gather(block, 'mp', axis=0, tiled=True)]
    all_gather x1, waiting for transfers between devices: 52.5 us -> 12.9 us  [per_device(): embed_parts = lax.all_gather(embed, 'mp', axis=0, tiled=False)]
    ppermute x0 -> x4, waiting for transfers between devices: none -> 36 us  [the longest x3 36 us: spread_weights(): lax.ppermute(own, 'seq', [(i, (i + 2 * step) % count) for i in range(coun...]
    all_to_all x1 -> x0, blocking collectives: 24.6 us -> none  [per_device(): lax.all_to_all(found.reshape(seq_count, capacity, -1), 'seq', split_axis=...]
    ppermute x1, waiting for transfers between devices: 19.1 us -> 0.01 us  [padded(): lax.ppermute(tail, axis, [(i, (i + 1) % count) for i in range(ends)])]
    all_to_all x0 -> x1, waiting for transfers between devices: none -> 16.5 us  [per_device(): lax.all_to_all(found.reshape(seq_count, capacity, -1), 'seq', split_axis=...]
  transfers between devices with their start and end apart: 15 -> 21, of which waited for: 12 -> 17; matrix products, arithmetic and copies ran while one was open for 7% -> 10% of each run, Pallas kernels for 0% -> 0%
where the time goes in v2:
time: 491 us; the launch traced here: 481 us
  waiting for transfers between devices  302 us (62%)
  matrix products  91 us (19%)
  other arithmetic  25.7 us (5%)
  starting transfers between devices  23.8 us (5%)
  local copies, waits for them, and re-layouts  16.4 us (3%)
  between operations  14.7 us (3%)
  blocking collectives  7.56 us (2%)
    unnamed x13, waiting for transfers between devices  110 us
    all_gather x2, waiting for transfers between devices, per_device(): lax.all_gather(block, 'mp', axis=0, tiled=True)  55.3 us
    all_gather x2, waiting for transfers between devices, per_device(): gathered.append(lax.all_gather(normed, 'mp', axis=0, tiled=True))  48.2 us
    ppermute x3, waiting for transfers between devices, spread_weights(): lax.ppermute(own, 'seq', [(i, (i + 2 * step) % count) for i in range(coun...  36 us
    sub x2, matrix products, masked_softmax(): raised = jnp.exp(scores - highest)  18 us
    all_to_all x1, waiting for transfers between devices, per_device(): lax.all_to_all(found.reshape(seq_count, capacity, -1), 'seq', split_axis=...  16.5 us
    dot_general x2, matrix products, per_device(): lax.dot_general(hidden, full_down, (((1,), (1,)), ((), ())), preferred_el...  15.1 us
    all_gather x1, waiting for transfers between devices, per_device(): embed_parts = lax.all_gather(embed, 'mp', axis=0, tiled=False)  12.9 us
  transfers between devices with their start and end apart: 21, of which 17 were waited for; matrix products, arithmetic and copies ran while one was open for 10% of the time, Pallas kernels for 0%

profile of v2, /device:TPU:3, one launch (start us, length us, event | category | flops | bytes accessed | tf_op | source)
XLA Modules:
  0.0 480.8 jit_solution(14202890111348135005)
XLA Ops:
  10.9 7.6 %all_to_all.11 = s32[8,1,256]{2,1,0:T(1,128)S(1)} all-to-all(s32[8,1,256]{2,1,0:T(1,128)S(1)} %bitcast.148), channel_id=1, replica_groups=mesh['seq'=8,'mp'=4] {'seq'}, dimensions={0} | all-to-all | bytes 16384 | tf_op jit(solution)/shard_map/all_to_all | solution.py:110
  18.5 6.4 %fusion.35 = bf16[2048,320]{0,1:T(8,128)(2,1)S(1)} fusion(bf16[4096,320]{0,1:T(8,128)(2,1)S(1)} %copy-done, s32[2048]{0:T(1024)S(1)} %bitcast.150), kind=kOutput, calls=%fused_computation.60 | convolution fusion | flops 5377753088 | bytes 3940352 | tf_op jit(solution)/shard_map/dot_general | solution.py:114
  26.0 5.0 %all-to-all-start.1 = ((bf16[8,256,320]{1,2,0:T(8,128)(2,1)}), bf16[8,256,320]{1,2,0:T(8,128)(2,1)S(1)}, u32[]{:S(2)}, u32[]{:S(2)}) async-start(bf16[8,256,320]{1,2,0:T(8,128)(2,1)} %bitcast.122), calls=%async_computation.1 | async-start | bytes 2621440 | tf_op jit(solution)/shard_map/all_to_all | solution.py:115
  31.2 16.5 %all-to-all-done.1 = bf16[8,256,320]{1,2,0:T(8,128)(2,1)S(1)} async-done(((bf16[8,256,320]{1,2,0:T(8,128)(2,1)}), bf16[8,256,320]{1,2,0:T(8,128)(2,1)S(1)}, u32[]{:S(2)}, u32[]{:S(2)}) %all-to-all-start.1) | async-done | bytes 1310752 | tf_op jit(solution)/shard_map/all_to_all | solution.py:115
  47.9 1.9 fusion.5
  51.3 2.6 collective-permute-start.1
  53.9 18.6 %collective-permute-done.3 = bf16[3,160,896]{2,1,0:T(8,128)(2,1)S(1)} collective-permute-done((bf16[3,160,896]{2,1,0:T(8,128)(2,1)S(1)}, bf16[3,160,896]{2,1,0:T(8,128)(2,1)S(1)}, u32[]{:S(2)}, u32[]{:S(2)}) %collective-permute-start.3) | collective-permute-done | bytes 860192 | tf_op jit(solution)/shard_map/ppermute | solution.py:51
  72.5 17.5 %collective-permute-done.2 = bf16[3,160,896]{2,1,0:T(8,128)(2,1)S(1)} collective-permute-done((bf16[3,160,896]{2,1,0:T(8,128)(2,1)S(1)}, bf16[3,160,896]{2,1,0:T(8,128)(2,1)S(1)}, u32[]{:S(2)}, u32[]{:S(2)}) %collective-permute-start.2) | collective-permute-done | bytes 860192 | tf_op jit(solution)/shard_map/ppermute | solution.py:51
  89.9 2.0 pad_maximum_fusion.1
  93.3 12.9 %all-gather.15.cloned.1.call-done = bf16[4096,320]{0,1:T(8,128)(2,1)} async-done(((bf16[1024,320]{0,1:T(8,128)(2,1)}), bf16[4096,320]{0,1:T(8,128)(2,1)}) %all-gather.15.cloned.1.call-update) | async-done | bytes 2621456 | tf_op jit(solution)/shard_map/all_gather | solution.py:127
  106.1 1.9 fusion.75
  110.5 2.5 select_bitcast_fusion
  115.0 2.6 fusion.74
  119.9 3.8 collective-permute-start.5
  126.9 4.3 collective-permute-done.5
  132.5 9.0 %fusion.79 = (f32[5,512]{1,0:T(8,128)S(1)}, f32[5,512,1024]{2,1,0:T(8,128)}) fusion(pred[512,1024]{1,0:T(8,128)(4,1)} %and_and_fusion, bf16[512,5,64]{0,2,1:T(8,128)(2,1)} %bitcast.144, bf16[1024,5,64]{0,2,1:T(8,128)(2,1)} %bitcast.142), kind=kOutput, calls=%fused_computation.178 | convolution fusion | flops 346031104 | bytes 12003328 | tf_op jit(solution)/shard_map/sub | solution.py:41
  141.5 6.0 %fusion.48 = bf16[5,64,512]{2,1,0:T(8,128)(2,1)S(1)} fusion(bf16[1024,5,64]{0,2,1:T(8,128)(2,1)} %bitcast.141, f32[5,512,1024]{2,1,0:T(8,128)} %get-tuple-element.54, f32[5,512]{1,0:T(8,128)S(1)} %get-tuple-element.53), kind=kOutput, calls=%fused_computation.92 | convolution fusion | flops 340951040 | bytes 11479040 | tf_op jit(solution)/shard_map/hqk,khd->qhd/dot_general | solution.py:172
  147.5 1.9 convolution_convert_fusion
  150.9 29.3 %reduce-scatter.15.cloned.1.call-done = bf16[128,1280]{1,0:T(8,128)(2,1)} async-done(((bf16[512,1280]{1,0:T(8,128)(2,1)}), bf16[128,1280]{1,0:T(8,128)(2,1)}) %reduce-scatter.15.cloned.1.call-update) | async-done | bytes 327696
  182.6 1.9 multiply_convert_fusion.5
  184.8 9.0 %fusion.80 = (f32[5,512]{1,0:T(8,128)S(1)}, f32[5,512,1024]{2,1,0:T(8,128)}) fusion(pred[512,1024]{1,0:T(8,128)(4,1)} %and_and_fusion.1, bf16[512,5,64]{0,2,1:T(8,128)(2,1)} %bitcast.143, bf16[1024,5,64]{0,2,1:T(8,128)(2,1)} %bitcast.133), kind=kOutput, calls=%fused_computation.179 | convolution fusion | flops 346031104 | bytes 12003328 | tf_op jit(solution)/shard_map/sub | solution.py:41
  193.8 5.8 %fusion.49 = bf16[5,64,512]{2,1,0:T(8,128)(2,1)S(1)} fusion(bf16[1024,5,64]{0,2,1:T(8,128)(2,1)S(1)} %bitcast.131, f32[5,512,1024]{2,1,0:T(8,128)} %get-tuple-element.56, f32[5,512]{1,0:T(8,128)S(1)} %get-tuple-element.55), kind=kOutput, calls=%fused_computation.93 | convolution fusion | flops 340951040 | bytes 11479040 | tf_op jit(solution)/shard_map/hqk,khd->qhd/dot_general | solution.py:172
  199.6 1.9 convolution_convert_fusion.1
  201.6 15.7 %all-gather.9.cloned.1.call-done = bf16[512,1280]{0,1:T(8,128)(2,1)} async-done(((bf16[128,1280]{0,1:T(8,128)(2,1)}), bf16[512,1280]{0,1:T(8,128)(2,1)}) %all-gather.9.cloned.1.call-update) | async-done | bytes 1310736 | tf_op jit(solution)/shard_map/all_gather | solution.py:186
  217.4 4.1 fusion.83
  221.5 7.6 %convolution_convert_fusion.2 = bf16[512,1280]{1,0:T(8,128)(2,1)} fusion(bf16[1280,896]{1,0:T(8,128)(2,1)} %bitcast.134, f32[512,896]{1,0:T(8,128)} %fusion.83, bf16[512,1280]{0,1:T(8,128)(2,1)} %all-gather.9.cloned.1.call-done, bf16[1280,896]{1,0:T(8,128)(2,1)} %bitcast.136), kind=kOutput, calls=%fused_computation.58 | convolution fusion | flops 2352218112 | bytes 9043968 | tf_op jit(solution)/shard_map/dot_general | solution.py:192
  229.2 19.7 %reduce-scatter.13.cloned.1.call-done = bf16[128,1280]{1,0:T(8,128)(2,1)} async-done(((bf16[512,1280]{1,0:T(8,128)(2,1)}), bf16[128,1280]{1,0:T(8,128)(2,1)}) %reduce-scatter.13.cloned.1.call-update) | async-done | bytes 327696
  248.9 1.9 copy.61
  250.8 30.3 %reduce-scatter.19.cloned.1.call-done = bf16[128,1280]{1,0:T(8,128)(2,1)} async-done(((bf16[512,1280]{1,0:T(8,128)(2,1)}), bf16[128,1280]{1,0:T(8,128)(2,1)}) %reduce-scatter.19.cloned.1.call-update) | async-done | bytes 327696
  283.6 2.3 multiply_convert_fusion.3
  287.3 32.5 %all-gather.7.cloned.1.call-done = bf16[512,1280]{0,1:T(8,128)(2,1)} async-done(((bf16[128,1280]{0,1:T(8,128)(2,1)}), bf16[512,1280]{0,1:T(8,128)(2,1)}) %all-gather.7.cloned.1.call-update) | async-done | bytes 1310736 | tf_op jit(solution)/shard_map/all_gather | solution.py:186
  319.8 4.1 fusion.82
  324.0 7.5 %convolution_convert_fusion.3 = bf16[512,1280]{1,0:T(8,128)(2,1)} fusion(bf16[1280,896]{1,0:T(8,128)(2,1)} %bitcast.135, f32[512,896]{1,0:T(8,128)} %fusion.82, bf16[512,1280]{0,1:T(8,128)(2,1)} %all-gather.7.cloned.1.call-done, bf16[1280,896]{1,0:T(8,128)(2,1)} %bitcast.137), kind=kOutput, calls=%fused_computation.59 | convolution fusion | flops 2352218112 | bytes 9043968 | tf_op jit(solution)/shard_map/dot_general | solution.py:192
  331.6 29.4 %reduce-scatter.17.cloned.1.call-done = bf16[128,1280]{1,0:T(8,128)(2,1)} async-done(((bf16[512,1280]{1,0:T(8,128)(2,1)}), bf16[128,1280]{1,0:T(8,128)(2,1)}) %reduce-scatter.17.cloned.1.call-update) | async-done | bytes 327696
  364.2 2.8 collective-permute-start
  367.0 3.0 collective-permute-done
  370.8 25.5 %all-gather.11.cloned.1.call-done = bf16[512,1280]{0,1:T(8,128)(2,1)} async-done(((bf16[128,1280]{0,1:T(8,128)(2,1)}), bf16[512,1280]{0,1:T(8,128)(2,1)}) %all-gather.11.cloned.1.call-update) | async-done | bytes 1310736 | tf_op jit(solution)/shard_map/all_gather | solution.py:201
  396.3 3.4 collective-permute-start.6
  400.1 29.8 %all-gather.13.cloned.1.call-done = bf16[512,1280]{0,1:T(8,128)(2,1)} async-done(((bf16[128,1280]{0,1:T(8,128)(2,1)}), bf16[512,1280]{0,1:T(8,128)(2,1)}) %all-gather.13.cloned.1.call-update) | async-done | bytes 1310736 | tf_op jit(solution)/shard_map/all_gather | solution.py:201
  429.9 2.5 collective-permute-start.7
  432.3 2.9 convolution_convert_fusion.12
  435.2 2.5 convolution_convert_fusion.13
  440.5 9.5 %collective-permute-done.7 = bf16[512,1280]{0,1:T(8,128)(2,1)S(1)} collective-permute-done((bf16[512,1280]{0,1:T(8,128)(2,1)}, bf16[512,1280]{0,1:T(8,128)(2,1)S(1)}, u32[]{:S(2)}, u32[]{:S(2)}) %collective-permute-start.7) | collective-permute-done | bytes 1310752 | tf_op jit(solution)/shard_map/ppermute | solution.py:27
  453.6 1.6 fusion.39
  459.9 2.8 fusion.50
  464.7 2.5 collective-permute-done.10
  467.2 3.8 collective-permute-done.9
  471.1 3.0 convolution_convert_fusion.14
  (155 shorter events, 44.4 us)
Async XLA Ops:
  6.5 11.9 %copy-start = (bf16[4096,320]{0,1:T(8,128)(2,1)S(1)}, bf16[4096,320]{0,1:T(8,128)(2,1)}, u32[]{:S(2)}) copy-start(bf16[4096,320]{0,1:T(8,128)(2,1)} %param.24) | copy-start | bytes 7864324
  24.9 6.2 %copy-start.12 = (bf16[896,160]{0,1:T(8,128)(2,1)S(1)}, bf16[896,160]{0,1:T(8,128)(2,1)}, u32[]{:S(2)}) copy-start(bf16[896,160]{0,1:T(8,128)(2,1)} %param.32) | copy-start | bytes 860164
  24.9 6.2 %copy-start.13 = (bf16[160,896]{1,0:T(8,128)(2,1)S(1)}, bf16[160,896]{1,0:T(8,128)(2,1)}, u32[]{:S(2)}) copy-start(bf16[160,896]{1,0:T(8,128)(2,1)} %param.31) | copy-start | bytes 860164
  24.9 6.2 %copy-start.14 = (bf16[160,896]{1,0:T(8,128)(2,1)S(1)}, bf16[160,896]{1,0:T(8,128)(2,1)}, u32[]{:S(2)}) copy-start(bf16[160,896]{1,0:T(8,128)(2,1)} %param.30) | copy-start | bytes 860164
  26.0 21.6 %all-to-all-start.1 = ((bf16[8,256,320]{1,2,0:T(8,128)(2,1)}), bf16[8,256,320]{1,2,0:T(8,128)(2,1)S(1)}, u32[]{:S(2)}, u32[]{:S(2)}) async-start(bf16[8,256,320]{1,2,0:T(8,128)(2,1)} %bitcast.122), calls=%async_computation.1 | async-start | bytes 2621440 | tf_op jit(solution)/shard_map/all_to_all | solution.py:115
  31.0 75.1 %all-gather.15.cloned.1.call-start = ((), (), s32[]{:S(2)}) async-start(), calls=%async_computation.10 | async-start | bytes 3276800 | tf_op jit(solution)/shard_map/all_gather | solution.py:127
  47.8 1.9 copy-start.15
  47.8 1.9 copy-start.17
  51.1 129.2 %reduce-scatter.15.cloned.1.call-start = ((), (), s32[]{:S(2)}) async-start(), calls=%async_computation.12 | async-start | bytes 1638400
  51.1 21.4 %collective-permute-start.3 = (bf16[3,160,896]{2,1,0:T(8,128)(2,1)S(1)}, bf16[3,160,896]{2,1,0:T(8,128)(2,1)S(1)}, u32[]{:S(2)}, u32[]{:S(2)}) collective-permute-start(bf16[3,160,896]{2,1,0:T(8,128)(2,1)S(1)} %pad_maximum_fusion.5), channel_id=1, source_target_pairs={{0,24},{4,28},{8,0},{12,4},{16,8},{20,12},{24,16},{28,20},{1,25},{... | collective-permute-start | bytes 2580488 | tf_op jit(solution)/shard_map/ppermute | solution.py:51
  51.2 38.8 %collective-permute-start.2 = (bf16[3,160,896]{2,1,0:T(8,128)(2,1)S(1)}, bf16[3,160,896]{2,1,0:T(8,128)(2,1)S(1)}, u32[]{:S(2)}, u32[]{:S(2)}) collective-permute-start(bf16[3,160,896]{2,1,0:T(8,128)(2,1)S(1)} %pad_maximum_fusion.5), channel_id=1, source_target_pairs={{0,16},{4,20},{8,24},{12,28},{16,0},{20,4},{24,8},{28,12},{1,17},{... | collective-permute-start | bytes 2580488 | tf_op jit(solution)/shard_map/ppermute | solution.py:51
  51.3 38.6 %collective-permute-start.1 = (bf16[3,160,896]{2,1,0:T(8,128)(2,1)S(1)}, bf16[3,160,896]{2,1,0:T(8,128)(2,1)S(1)}, u32[]{:S(2)}, u32[]{:S(2)}) collective-permute-start(bf16[3,160,896]{2,1,0:T(8,128)(2,1)S(1)} %pad_maximum_fusion.5), channel_id=1, source_target_pairs={{0,8},{4,12},{8,16},{12,20},{16,24},{20,28},{24,0},{28,4},{1,9},{5... | collective-permute-start | bytes 2580488 | tf_op jit(solution)/shard_map/ppermute | solution.py:51
  89.9 3.3 copy-start.16
  91.9 18.6 %collective-permute-start.4 = (bf16[4,3,160,896]{3,2,0,1:T(8,128)(2,1)}, bf16[4,3,160,896]{3,2,0,1:T(8,128)(2,1)}, u32[]{:S(2)}, u32[]{:S(2)}) collective-permute-start(bf16[4,3,160,896]{3,2,0,1:T(8,128)(2,1)} %pad_maximum_fusion.1), channel_id=1, source_target_pairs={{0,4},{4,0},{8,12},{12,8},{16,20},{20,16},{24,28},{28,24},{1,5},{5... | collective-permute-start | bytes 10321928 | tf_op jit(solution)/shard_map/ppermute | solution.py:53
  108.9 1.6 copy-start.2
  115.0 2.6 copy-start.22
  118.8 12.5 %copy-start.5 = (bf16[1024,320]{0,1:T(8,128)(2,1)}, bf16[1024,320]{0,1:T(8,128)(2,1)S(1)}, u32[]{:S(2)}) copy-start(bf16[1024,320]{0,1:T(8,128)(2,1)S(1)} %convolution_convert_fusion.7) | copy-start | bytes 1966084
  119.8 5.2 %copy-start.24 = (bf16[1280,320]{0,1:T(8,128)(2,1)S(1)}, bf16[1280,320]{0,1:T(8,128)(2,1)}, u32[]{:S(2)}) copy-start(bf16[1280,320]{0,1:T(8,128)(2,1)} %param.26) | copy-start | bytes 2457604
  119.9 11.3 %collective-permute-start.5 = (bf16[2,512,320]{1,2,0:T(8,128)(2,1)S(1)}, bf16[2,512,320]{1,2,0:T(8,128)(2,1)S(1)}, u32[]{:S(2)}, u32[]{:S(2)}) collective-permute-start(bf16[2,512,320]{1,2,0:T(8,128)(2,1)S(1)} %pad_maximum_fusion.8), channel_id=1, source_target_pairs={{0,4},{4,8},{8,12},{12,16},{16,20},{20,24},{24,28},{1,5},{5,9},{9,... | collective-permute-start | bytes 1966088 | tf_op jit(solution)/shard_map/ppermute | solution.py:14
  141.5 6.0 %copy-start.25 = (bf16[320,1280]{1,0:T(8,128)(2,1)S(1)}, bf16[320,1280]{1,0:T(8,128)(2,1)}, u32[]{:S(2)}) copy-start(bf16[320,1280]{1,0:T(8,128)(2,1)} %param.29) | copy-start | bytes 2457604
  149.5 67.8 %all-gather.9.cloned.1.call-start = ((), (), s32[]{:S(2)}) async-start(), calls=%async_computation.7 | async-start | bytes 1638400 | tf_op jit(solution)/shard_map/all_gather | solution.py:186
  184.6 64.3 %reduce-scatter.13.cloned.1.call-start = ((), (), s32[]{:S(2)}) async-start(), calls=%async_computation.11 | async-start | bytes 1638400
  193.8 5.8 %copy-start.26 = (bf16[320,1280]{1,0:T(8,128)(2,1)S(1)}, bf16[320,1280]{1,0:T(8,128)(2,1)}, u32[]{:S(2)}) copy-start(bf16[320,1280]{1,0:T(8,128)(2,1)} %param.29) | copy-start | bytes 2457604
  201.6 79.5 %reduce-scatter.19.cloned.1.call-start = ((), (), s32[]{:S(2)}) async-start(), calls=%async_computation.14 | async-start | bytes 1638400
  229.1 90.7 %all-gather.7.cloned.1.call-start = ((), (), s32[]{:S(2)}) async-start(), calls=%async_computation.6 | async-start | bytes 1638400 | tf_op jit(solution)/shard_map/all_gather | solution.py:186
  282.3 1.3 copy-start.4
  287.0 73.9 %reduce-scatter.17.cloned.1.call-start = ((), (), s32[]{:S(2)}) async-start(), calls=%async_computation.13 | async-start | bytes 1638400
  331.5 32.7 %copy-start.18 = (s32[32]{0:T(128)S(1)}, s32[32]{0:T(128)}, u32[]{:S(2)}) copy-start(s32[32]{0:T(128)} %param.22) | copy-start | bytes 388
  331.5 64.8 %all-gather.11.cloned.1.call-start = ((), (), s32[]{:S(2)}) async-start(), calls=%async_computation.8 | async-start | bytes 1638400 | tf_op jit(solution)/shard_map/all_gather | solution.py:201
  363.4 66.4 %all-gather.13.cloned.1.call-start = ((), (), s32[]{:S(2)}) async-start(), calls=%async_computation.9 | async-start | bytes 1638400 | tf_op jit(solution)/shard_map/all_gather | solution.py:201
  364.2 5.9 %collective-permute-start = (s32[1]{0:T(128)S(1)}, s32[1]{0:T(128)}, u32[]{:S(2)}, u32[]{:S(2)}) collective-permute-start(s32[1]{0:T(128)S(1)} %bitcast.154), channel_id=1, source_target_pairs={{4,0},{8,4},{12,8},{16,12},{20,16},{24,20},{28,24},{5,1},{9,5},{13... | collective-permute-start | bytes 20 | tf_op jit(solution)/shard_map/ppermute | solution.py:14
  396.3 44.1 %collective-permute-start.6 = (bf16[512,1280]{0,1:T(8,128)(2,1)}, bf16[512,1280]{0,1:T(8,128)(2,1)S(1)}, u32[]{:S(2)}, u32[]{:S(2)}) collective-permute-start(bf16[512,1280]{0,1:T(8,128)(2,1)} %all-gather.11.cloned.1.call-done), channel_id=1, source_target_pairs={{0,4},{4,8},{8,12},{12,16},{16,20},{20,24},{24,28},{1,5},{5,9},{9,... | collective-permute-start | bytes 3932168 | tf_op jit(solution)/shard_map/ppermute | solution.py:25
  400.0 37.7 %copy-start.19 = (bf16[512,1280]{0,1:T(8,128)(2,1)S(1)}, bf16[512,1280]{0,1:T(8,128)(2,1)}, u32[]{:S(2)}) copy-start(bf16[512,1280]{0,1:T(8,128)(2,1)} %all-gather.11.cloned.1.call-done) | copy-start | bytes 3932164
  429.9 5.4 %copy-start.21 = (bf16[512,1280]{0,1:T(8,128)(2,1)S(1)}, bf16[512,1280]{0,1:T(8,128)(2,1)}, u32[]{:S(2)}) copy-start(bf16[512,1280]{0,1:T(8,128)(2,1)} %all-gather.13.cloned.1.call-done) | copy-start | bytes 3932164
  429.9 7.9 %copy-start.28 = (bf16[1280,320]{0,1:T(8,128)(2,1)S(1)}, bf16[1280,320]{0,1:T(8,128)(2,1)}, u32[]{:S(2)}) copy-start(bf16[1280,320]{0,1:T(8,128)(2,1)} %param.34) | copy-start | bytes 2457604
  429.9 20.2 %collective-permute-start.7 = (bf16[512,1280]{0,1:T(8,128)(2,1)}, bf16[512,1280]{0,1:T(8,128)(2,1)S(1)}, u32[]{:S(2)}, u32[]{:S(2)}) collective-permute-start(bf16[512,1280]{0,1:T(8,128)(2,1)} %all-gather.13.cloned.1.call-done), channel_id=1, source_target_pairs={{4,0},{8,4},{12,8},{16,12},{20,16},{24,20},{28,24},{5,1},{9,5},{13... | collective-permute-start | bytes 3932168 | tf_op jit(solution)/shard_map/ppermute | solution.py:27
  440.3 9.9 %copy-start.27 = (bf16[1280,320]{0,1:T(8,128)(2,1)S(1)}, bf16[1280,320]{0,1:T(8,128)(2,1)}, u32[]{:S(2)}) copy-start(bf16[1280,320]{0,1:T(8,128)(2,1)} %param.35) | copy-start | bytes 2457604
  452.3 1.3 copy-start.20
  453.6 1.6 copy-start.7
  453.6 2.1 copy-start.11
  455.2 1.6 copy-start.8
  456.8 1.8 copy-start.9
  456.9 1.8 copy-start.10
  459.9 3.0 copy-start.6
  459.9 14.2 %copy-start.1 = (bf16[4096,320]{0,1:T(8,128)(2,1)S(1)}, bf16[4096,320]{0,1:T(8,128)(2,1)}, u32[]{:S(2)}) copy-start(bf16[4096,320]{0,1:T(8,128)(2,1)} %param.24) | copy-start | bytes 7864324
  463.1 4.1 collective-permute-start.10
  463.8 7.3 %collective-permute-start.9 = (bf16[32,1280]{1,0:T(8,128)(2,1)S(1)}, bf16[32,1280]{1,0:T(8,128)(2,1)S(1)}, u32[]{:S(2)}, u32[]{:S(2)}) collective-permute-start(bf16[32,1280]{1,0:T(8,128)(2,1)S(1)} %convolution_convert_fusion.4), channel_id=1, source_target_pairs={{0,2},{1,3},{2,0},{3,1},{4,6},{5,7},{6,4},{7,5},{8,10},{9,11},{10,... | collective-permute-start | bytes 245768 | tf_op jit(solution)/shard_map/ppermute | solution.py:270
  463.8 7.3 %collective-permute-start.8 = (bf16[32,1280]{1,0:T(8,128)(2,1)S(1)}, bf16[32,1280]{1,0:T(8,128)(2,1)S(1)}, u32[]{:S(2)}, u32[]{:S(2)}) collective-permute-start(bf16[32,1280]{1,0:T(8,128)(2,1)S(1)} %convolution_convert_fusion.4), channel_id=1, source_target_pairs={{0,1},{1,2},{2,3},{3,0},{4,5},{5,6},{6,7},{7,4},{8,9},{9,10},{10,1... | collective-permute-start | bytes 245768 | tf_op jit(solution)/shard_map/ppermute | solution.py:270
  (2 other events, 2.2 us)
Sparse Core Ops, SparseCore 0:
  51.2 54.8 all-gather.14
  149.6 30.5 reduce-scatter.14
  184.7 32.6 all-gather.8
  219.5 29.3 reduce-scatter.12
  251.0 29.9 reduce-scatter.18
  287.2 32.6 all-gather.6
  331.6 29.3 reduce-scatter.16
  363.6 32.6 all-gather.10
  397.8 31.9 all-gather.12

commit v3 on v2

--- a/solution.py
+++ b/solution.py
@@ -63,6 +63,10 @@
         ordered[:, :, part].reshape(count * own.shape[1], own.shape[2])
         for part in range(own.shape[0])
     ]
+
+
+def after(value, *others):
+    return lax.optimization_barrier((value, *others))[0]
 
 
 def per_device(
@@ -148,6 +152,8 @@
     key_span = jnp.concatenate([earlier_pair[0], keys], axis=0)
     value_span = jnp.concatenate([earlier_pair[1], values], axis=0)
     first = position * length
+    terms = []
+    scattered = []
     for block in range(length // WINDOW):
         query_block = queries[block * WINDOW : (block + 1) * WINDOW].reshape(
             WINDOW, local_heads, HD
@@ -158,6 +164,7 @@
         value_block = value_span[block * WINDOW : block * WINDOW + 2 * WINDOW].reshape(
             2 * WINDOW, local_heads, HD
         )
+        query_block = after(query_block, *terms[-1:])
         query_pos = first + block * WINDOW + jnp.arange(WINDOW, dtype=jnp.int32)
         key_pos = first + (block - 1) * WINDOW + jnp.arange(2 * WINDOW, dtype=jnp.int32)
         valid = (
@@ -173,45 +180,55 @@
             "hqk,khd->qhd", weights, value_block, preferred_element_type=jnp.float32
         ).astype(jnp.bfloat16)
         heads_out = mixed_block.reshape(WINDOW, local_width)
-        attn_terms = jnp.dot(heads_out, w_attn_out, preferred_element_type=jnp.float32)
-        residuals[block] = residuals[block] + lax.psum_scatter(
-            attn_terms.astype(jnp.bfloat16), "mp", scatter_dimension=0, tiled=True
-        ).astype(jnp.float32)
+        attn_terms = jnp.dot(
+            heads_out, w_attn_out, preferred_element_type=jnp.float32
+        ).astype(jnp.bfloat16)
+        terms.append(attn_terms)
+        scattered.append(
+            lax.psum_scatter(attn_terms, "mp", scatter_dimension=0, tiled=True)
+        )
     gathered = []
+    norms = []
     for block, residual in enumerate(residuals):
-        if block > 0:
-            residual, normed = lax.optimization_barrier((residual, normed))
-            residuals[block] = residual
-        normed = rms_scale(residual, norm_gains[1]).astype(jnp.bfloat16)
-        gathered.append(lax.all_gather(normed, "mp", axis=0, tiled=True))
-    encoded_blocks = []
-    for block, (residual, mlp_in) in enumerate(zip(residuals, gathered)):
+        mixed = after(scattered[block], terms[-1], *norms[-1:])
+        residuals[block] = residual + mixed.astype(jnp.float32)
+        norms.append(rms_scale(residuals[block], norm_gains[1]).astype(jnp.bfloat16))
+        gathered.append(lax.all_gather(norms[block], "mp", axis=0, tiled=True))
+    terms = []
+    scattered = []
+    for mlp_in in gathered:
+        mlp_in = after(mlp_in, norms[-1], *terms[-1:])
         gate = jnp.dot(mlp_in, full_gate, preferred_element_type=jnp.float32)
         lifted = jnp.dot(mlp_in, full_up, preferred_element_type=jnp.float32)
         hidden = (jax.nn.silu(gate) * lifted).astype(jnp.bfloat16)
         down_terms = lax.dot_general(
             hidden, full_down, (((1,), (1,)), ((), ())), preferred_element_type=jnp.float32
-        )
-        residual = residual + lax.psum_scatter(
-            down_terms.astype(jnp.bfloat16), "mp", scatter_dimension=0, tiled=True
-        ).astype(jnp.float32)
-        if block > 0:
-            residual, encoded_blocks[-1] = lax.optimization_barrier((residual, encoded_blocks[-1]))
+        ).astype(jnp.bfloat16)
+        terms.append(down_terms)
+        scattered.append(
+            lax.psum_scatter(down_terms, "mp", scatter_dimension=0, tiled=True)
+        )
+    encoded_blocks = []
+    for residual, mixed in zip(residuals, scattered):
+        mixed = after(mixed, terms[-1], *encoded_blocks[-1:])
+        residual = residual + mixed.astype(jnp.float32)
         encoded_blocks.append(rms_scale(residual, norm_gains[2]).astype(jnp.bfloat16))
-    state_blocks = [lax.all_gather(block, "mp", axis=0, tiled=True) for block in encoded_blocks]
+    state_blocks = []
+    key_parts = []
+    value_parts = []
+    for block in encoded_blocks:
+        state = lax.all_gather(block, "mp", axis=0, tiled=True)
+        state = after(state, encoded_blocks[-1], *key_parts[-1:], *value_parts[-1:])
+        state_blocks.append(state)
+        key_parts.append(
+            jnp.dot(state, w_cross_key, preferred_element_type=jnp.float32).astype(jnp.bfloat16)
+        )
+        value_parts.append(
+            jnp.dot(state, w_cross_value, preferred_element_type=jnp.float32).astype(jnp.bfloat16)
+        )
     states = jnp.concatenate(state_blocks, axis=0)
-    cross_keys = jnp.concatenate(
-        [
-            jnp.dot(block, w_cross_key, preferred_element_type=jnp.float32).astype(jnp.bfloat16)
-            for block in state_blocks
-        ]
-    )
-    cross_values = jnp.concatenate(
-        [
-            jnp.dot(block, w_cross_value, preferred_element_type=jnp.float32).astype(jnp.bfloat16)
-            for block in state_blocks
-        ]
-    )
+    cross_keys = jnp.concatenate(key_parts, axis=0)
+    cross_values = jnp.concatenate(value_parts, axis=0)
     following = passed_along(patch_start[:1], "seq", -1)
     last_end = jnp.where(position == seq_count - 1, seq_count * length, following[0])
     patch_end = jnp.concatenate([patch_start[1:], last_end[None]])

time: 491 us -> 490 us (level)
  waiting for transfers between devices: 302 us -> 294 us
  matrix products: 91 us -> 97.6 us
    unnamed x13, waiting for transfers between devices: 110 us -> 88.1 us
    ppermute x1, waiting for transfers between devices: 0.01 us -> 16.9 us  [padded(): lax.ppermute(tail, axis, [(i, (i + 1) % count) for i in range(ends)])]
    all_gather x4, waiting for transfers between devices: 104 us -> 109 us  [the longest x2 57.1 us: per_device(): state = lax.all_gather(block, 'mp', axis=0, tiled=True)]
    optimization_barrier x0 -> x4, local copies, waits for them, and re-layouts: none -> 5.43 us  [after(): return lax.optimization_barrier((value, *others))[0]]
    unnamed x63 -> x69, local copies, waits for them, and re-layouts: 9.01 us -> 4.03 us
  transfers between devices with their start and end apart: 21 -> 21, of which waited for: 17 -> 17; matrix products, arithmetic and copies ran while one was open for 10% -> 16% of each run, Pallas kernels for 0% -> 0%
where the time goes in v3:
time: 490 us; the launch traced here: 480 us
  waiting for transfers between devices  294 us (60%)
  matrix products  97.6 us (20%)
  other arithmetic  24.4 us (5%)
  starting transfers between devices  23.5 us (5%)
  local copies, waits for them, and re-layouts  18.4 us (4%)
  between operations  14.7 us (3%)
  blocking collectives  7.56 us (2%)
    unnamed x13, waiting for transfers between devices  88.1 us
    all_gather x2, waiting for transfers between devices, per_device(): state = lax.all_gather(block, 'mp', axis=0, tiled=True)  57.1 us
    all_gather x2, waiting for transfers between devices, per_device(): gathered.append(lax.all_gather(norms[block], 'mp', axis=0, tiled=True))  52.3 us
    ppermute x3, waiting for transfers between devices, spread_weights(): lax.ppermute(own, 'seq', [(i, (i + 2 * step) % count) for i in range(coun...  36.2 us
    sub x2, matrix products, masked_softmax(): raised = jnp.exp(scores - highest)  18 us
    ppermute x1, waiting for transfers between devices, padded(): lax.ppermute(tail, axis, [(i, (i + 1) % count) for i in range(ends)])  16.9 us
    all_to_all x1, waiting for transfers between devices, per_device(): lax.all_to_all(found.reshape(seq_count, capacity, -1), 'seq', split_axis=...  16.5 us
    dot_general x2, matrix products, per_device(): lax.dot_general(hidden, full_down, (((1,), (1,)), ((), ())), preferred_el...  15.4 us
  transfers between devices with their start and end apart: 21, of which 17 were waited for; matrix products, arithmetic and copies ran while one was open for 16% of the time, Pallas kernels for 0%

profile of v3, /device:TPU:3, one launch (start us, length us, event | category | flops | bytes accessed | tf_op | source)
XLA Modules:
  0.0 480.3 jit_solution(15882749877517537363)
XLA Ops:
  10.9 7.6 %all_to_all.11 = s32[8,1,256]{2,1,0:T(1,128)S(1)} all-to-all(s32[8,1,256]{2,1,0:T(1,128)S(1)} %bitcast.147), channel_id=1, replica_groups=mesh['seq'=8,'mp'=4] {'seq'}, dimensions={0} | all-to-all | bytes 16384 | tf_op jit(solution)/shard_map/all_to_all | solution.py:114
  18.5 6.4 %fusion.35 = bf16[2048,320]{0,1:T(8,128)(2,1)S(1)} fusion(bf16[4096,320]{0,1:T(8,128)(2,1)S(1)} %copy-done, s32[2048]{0:T(1024)S(1)} %bitcast.149), kind=kOutput, calls=%fused_computation.60 | convolution fusion | flops 5377753088 | bytes 3940352 | tf_op jit(solution)/shard_map/dot_general | solution.py:118
  26.1 5.0 %all-to-all-start.1 = ((bf16[8,256,320]{1,2,0:T(8,128)(2,1)}), bf16[8,256,320]{1,2,0:T(8,128)(2,1)S(1)}, u32[]{:S(2)}, u32[]{:S(2)}) async-start(bf16[8,256,320]{1,2,0:T(8,128)(2,1)} %bitcast.115), calls=%async_computation.1 | async-start | bytes 2621440 | tf_op jit(solution)/shard_map/all_to_all | solution.py:119
  31.2 16.5 %all-to-all-done.1 = bf16[8,256,320]{1,2,0:T(8,128)(2,1)S(1)} async-done(((bf16[8,256,320]{1,2,0:T(8,128)(2,1)}), bf16[8,256,320]{1,2,0:T(8,128)(2,1)S(1)}, u32[]{:S(2)}, u32[]{:S(2)}) %all-to-all-start.1) | async-done | bytes 1310752 | tf_op jit(solution)/shard_map/all_to_all | solution.py:119
  47.9 1.9 fusion.5
  51.3 2.5 collective-permute-start.1
  53.8 18.7 %collective-permute-done.3 = bf16[3,160,896]{2,1,0:T(8,128)(2,1)S(1)} collective-permute-done((bf16[3,160,896]{2,1,0:T(8,128)(2,1)S(1)}, bf16[3,160,896]{2,1,0:T(8,128)(2,1)S(1)}, u32[]{:S(2)}, u32[]{:S(2)}) %collective-permute-start.3) | collective-permute-done | bytes 860192 | tf_op jit(solution)/shard_map/ppermute | solution.py:51
  72.5 17.5 %collective-permute-done.2 = bf16[3,160,896]{2,1,0:T(8,128)(2,1)S(1)} collective-permute-done((bf16[3,160,896]{2,1,0:T(8,128)(2,1)S(1)}, bf16[3,160,896]{2,1,0:T(8,128)(2,1)S(1)}, u32[]{:S(2)}, u32[]{:S(2)}) %collective-permute-start.2) | collective-permute-done | bytes 860192 | tf_op jit(solution)/shard_map/ppermute | solution.py:51
  90.0 2.2 pad_maximum_fusion.1
  93.6 12.5 %all-gather.15.cloned.1.call-done = bf16[4096,320]{0,1:T(8,128)(2,1)} async-done(((bf16[1024,320]{0,1:T(8,128)(2,1)}), bf16[4096,320]{0,1:T(8,128)(2,1)}) %all-gather.15.cloned.1.call-update) | async-done | bytes 2621456 | tf_op jit(solution)/shard_map/all_gather | solution.py:131
  106.2 1.9 fusion.75
  110.8 2.5 select_bitcast_fusion
  115.4 3.0 fusion.74
  121.4 3.6 collective-permute-start.5
  126.4 3.0 convolution_convert_fusion.8
  130.4 2.5 collective-permute-done.5
  135.3 9.0 %fusion.79 = (f32[5,512]{1,0:T(8,128)S(1)}, f32[5,512,1024]{2,1,0:T(8,128)}) fusion(pred[512,1024]{1,0:T(8,128)(4,1)} %and_and_fusion, bf16[512,5,64]{0,2,1:T(8,128)(2,1)} %bitcast.143, bf16[1024,5,64]{0,2,1:T(8,128)(2,1)} %bitcast.141), kind=kOutput, calls=%fused_computation.178 | convolution fusion | flops 346031104 | bytes 12003328 | tf_op jit(solution)/shard_map/sub | solution.py:41
  144.3 6.0 %fusion.49 = bf16[5,64,512]{2,1,0:T(8,128)(2,1)S(1)} fusion(bf16[1024,5,64]{0,2,1:T(8,128)(2,1)} %bitcast.140, f32[5,512,1024]{2,1,0:T(8,128)} %get-tuple-element.64, f32[5,512]{1,0:T(8,128)S(1)} %get-tuple-element.63), kind=kOutput, calls=%fused_computation.93 | convolution fusion | flops 340951040 | bytes 11479040 | tf_op jit(solution)/shard_map/hqk,khd->qhd/dot_general | solution.py:179
  150.3 2.0 convolution_convert_fusion.1
  154.1 9.0 %fusion.80 = (f32[5,512]{1,0:T(8,128)S(1)}, f32[5,512,1024]{2,1,0:T(8,128)}) fusion(pred[512,1024]{1,0:T(8,128)(4,1)} %and_and_fusion.1, bf16[512,5,64]{0,2,1:T(8,128)(2,1)} %bitcast.142, bf16[1024,5,64]{0,2,1:T(8,128)(2,1)} %bitcast.132), kind=kOutput, calls=%fused_computation.179 | convolution fusion | flops 346031104 | bytes 12003328 | tf_op jit(solution)/shard_map/sub | solution.py:41
  163.1 5.9 %fusion.48 = bf16[5,64,512]{2,1,0:T(8,128)(2,1)S(1)} fusion(bf16[1024,5,64]{0,2,1:T(8,128)(2,1)S(1)} %bitcast.130, f32[5,512,1024]{2,1,0:T(8,128)} %get-tuple-element.66, f32[5,512]{1,0:T(8,128)S(1)} %get-tuple-element.65), kind=kOutput, calls=%fused_computation.92 | convolution fusion | flops 340951040 | bytes 11479040 | tf_op jit(solution)/shard_map/hqk,khd->qhd/dot_general | solution.py:179
  169.0 2.0 convolution_convert_fusion
  171.1 12.0 %reduce-scatter.15.cloned.1.call-done = bf16[128,1280]{1,0:T(8,128)(2,1)} async-done(((bf16[512,1280]{1,0:T(8,128)(2,1)}), bf16[128,1280]{1,0:T(8,128)(2,1)}) %reduce-scatter.15.cloned.1.call-update) | async-done | bytes 327696
  185.5 29.9 %reduce-scatter.13.cloned.1.call-done = bf16[128,1280]{1,0:T(8,128)(2,1)} async-done(((bf16[512,1280]{1,0:T(8,128)(2,1)}), bf16[128,1280]{1,0:T(8,128)(2,1)}) %reduce-scatter.13.cloned.1.call-update) | async-done | bytes 327696
  217.9 31.6 %all-gather.9.cloned.1.call-done = bf16[512,1280]{0,1:T(8,128)(2,1)} async-done(((bf16[128,1280]{0,1:T(8,128)(2,1)}), bf16[512,1280]{0,1:T(8,128)(2,1)}) %all-gather.9.cloned.1.call-update) | async-done | bytes 1310736 | tf_op jit(solution)/shard_map/all_gather | solution.py:196
  249.5 4.8 %fusion.82 = f32[512,896]{1,0:T(8,128)} fusion(bf16[512,1280]{0,1:T(8,128)(2,1)} %all-gather.9.cloned.1.call-done, bf16[1280,896]{1,0:T(8,128)(2,1)} %bitcast.117), kind=kOutput, calls=%fused_computation.181 | convolution fusion | flops 1174405120 | bytes 5439488 | tf_op jit(solution)/shard_map/dot_general | solution.py:201
  254.4 7.7 %convolution_convert_fusion.3 = bf16[512,1280]{1,0:T(8,128)(2,1)} fusion(bf16[1280,896]{1,0:T(8,128)(2,1)} %bitcast.133, f32[512,896]{1,0:T(8,128)} %fusion.82, bf16[512,1280]{0,1:T(8,128)(2,1)} %all-gather.9.cloned.1.call-done, bf16[1280,896]{1,0:T(8,128)(2,1)} %bitcast.135), kind=kOutput, calls=%fused_computation.59 | convolution fusion | flops 2352218112 | bytes 9043968 | tf_op jit(solution)/shard_map/dot_general | solution.py:204
  262.3 20.6 %all-gather.7.cloned.1.call-done = bf16[512,1280]{0,1:T(8,128)(2,1)} async-done(((bf16[128,1280]{0,1:T(8,128)(2,1)}), bf16[512,1280]{0,1:T(8,128)(2,1)}) %all-gather.7.cloned.1.call-update) | async-done | bytes 1310736 | tf_op jit(solution)/shard_map/all_gather | solution.py:196
  282.9 4.8 %fusion.83 = f32[512,896]{1,0:T(8,128)} fusion(bf16[512,1280]{0,1:T(8,128)(2,1)} %all-gather.7.cloned.1.call-done, bf16[1280,896]{1,0:T(8,128)(2,1)} %bitcast.118), kind=kOutput, calls=%fused_computation.182 | convolution fusion | flops 1174405120 | bytes 5439488 | tf_op jit(solution)/shard_map/dot_general | solution.py:201
  287.8 7.8 %convolution_convert_fusion.2 = bf16[512,1280]{1,0:T(8,128)(2,1)} fusion(bf16[1280,896]{1,0:T(8,128)(2,1)} %bitcast.134, f32[512,896]{1,0:T(8,128)} %fusion.83, bf16[512,1280]{0,1:T(8,128)(2,1)} %all-gather.7.cloned.1.call-done, bf16[1280,896]{1,0:T(8,128)(2,1)} %bitcast.136), kind=kOutput, calls=%fused_computation.58 | convolution fusion | flops 2352218112 | bytes 9043968 | tf_op jit(solution)/shard_map/dot_general | solution.py:204
  295.6 18.9 %reduce-scatter.19.cloned.1.call-done = bf16[128,1280]{1,0:T(8,128)(2,1)} async-done(((bf16[512,1280]{1,0:T(8,128)(2,1)}), bf16[128,1280]{1,0:T(8,128)(2,1)}) %reduce-scatter.19.cloned.1.call-update) | async-done | bytes 327696
  314.5 1.9 copy.67
  317.5 2.0 multiply_convert_fusion.3
  319.6 27.2 %reduce-scatter.17.cloned.1.call-done = bf16[128,1280]{1,0:T(8,128)(2,1)} async-done(((bf16[512,1280]{1,0:T(8,128)(2,1)}), bf16[128,1280]{1,0:T(8,128)(2,1)}) %reduce-scatter.17.cloned.1.call-update) | async-done | bytes 327696
  349.2 2.8 collective-permute-start
  352.1 29.0 %all-gather.13.cloned.1.call-done = bf16[512,1280]{0,1:T(8,128)(2,1)} async-done(((bf16[128,1280]{0,1:T(8,128)(2,1)}), bf16[512,1280]{0,1:T(8,128)(2,1)}) %all-gather.13.cloned.1.call-update) | async-done | bytes 1310736 | tf_op jit(solution)/shard_map/all_gather | solution.py:220
  381.0 3.0 convolution_convert_fusion.13
  384.0 2.5 convolution_convert_fusion.12
  386.5 28.1 %all-gather.11.cloned.1.call-done = bf16[512,1280]{0,1:T(8,128)(2,1)} async-done(((bf16[128,1280]{0,1:T(8,128)(2,1)}), bf16[512,1280]{0,1:T(8,128)(2,1)}) %all-gather.11.cloned.1.call-update) | async-done | bytes 1310736 | tf_op jit(solution)/shard_map/all_gather | solution.py:220
  414.6 3.4 collective-permute-start.6
  418.8 2.0 collective-permute-start.7
  421.2 2.9 convolution_convert_fusion.11
  424.1 2.4 convolution_convert_fusion.10
  426.5 16.9 %collective-permute-done.6 = bf16[512,1280]{0,1:T(8,128)(2,1)S(1)} collective-permute-done((bf16[512,1280]{0,1:T(8,128)(2,1)}, bf16[512,1280]{0,1:T(8,128)(2,1)S(1)}, u32[]{:S(2)}, u32[]{:S(2)}) %collective-permute-start.6) | collective-permute-done | bytes 1310752 | tf_op jit(solution)/shard_map/ppermute | solution.py:25
  443.6 4.9 %collective-permute-done.7 = bf16[512,1280]{0,1:T(8,128)(2,1)S(1)} collective-permute-done((bf16[512,1280]{0,1:T(8,128)(2,1)S(1)}, bf16[512,1280]{0,1:T(8,128)(2,1)S(1)}, u32[]{:S(2)}, u32[]{:S(2)}) %collective-permute-start.7) | collective-permute-done | bytes 1310752 | tf_op jit(solution)/shard_map/ppermute | solution.py:27
  458.5 2.8 fusion.50
  465.2 5.3 %collective-permute-done.9 = bf16[32,1280]{1,0:T(8,128)(2,1)S(1)} collective-permute-done((bf16[32,1280]{1,0:T(8,128)(2,1)S(1)}, bf16[32,1280]{1,0:T(8,128)(2,1)S(1)}, u32[]{:S(2)}, u32[]{:S(2)}) %collective-permute-start.9) | collective-permute-done | bytes 81952 | tf_op jit(solution)/shard_map/ppermute | solution.py:287
  470.5 3.0 convolution_convert_fusion.14
  (163 shorter events, 46.2 us)
Async XLA Ops:
  6.5 11.9 %copy-start = (bf16[4096,320]{0,1:T(8,128)(2,1)S(1)}, bf16[4096,320]{0,1:T(8,128)(2,1)}, u32[]{:S(2)}) copy-start(bf16[4096,320]{0,1:T(8,128)(2,1)} %param.24) | copy-start | bytes 7864324
  24.9 6.2 %copy-start.18 = (bf16[896,160]{0,1:T(8,128)(2,1)S(1)}, bf16[896,160]{0,1:T(8,128)(2,1)}, u32[]{:S(2)}) copy-start(bf16[896,160]{0,1:T(8,128)(2,1)} %param.32) | copy-start | bytes 860164
  24.9 6.2 %copy-start.19 = (bf16[160,896]{1,0:T(8,128)(2,1)S(1)}, bf16[160,896]{1,0:T(8,128)(2,1)}, u32[]{:S(2)}) copy-start(bf16[160,896]{1,0:T(8,128)(2,1)} %param.31) | copy-start | bytes 860164
  24.9 6.2 %copy-start.20 = (bf16[160,896]{1,0:T(8,128)(2,1)S(1)}, bf16[160,896]{1,0:T(8,128)(2,1)}, u32[]{:S(2)}) copy-start(bf16[160,896]{1,0:T(8,128)(2,1)} %param.30) | copy-start | bytes 860164
  26.1 21.6 %all-to-all-start.1 = ((bf16[8,256,320]{1,2,0:T(8,128)(2,1)}), bf16[8,256,320]{1,2,0:T(8,128)(2,1)S(1)}, u32[]{:S(2)}, u32[]{:S(2)}) async-start(bf16[8,256,320]{1,2,0:T(8,128)(2,1)} %bitcast.115), calls=%async_computation.1 | async-start | bytes 2621440 | tf_op jit(solution)/shard_map/all_to_all | solution.py:119
  31.0 75.1 %all-gather.15.cloned.1.call-start = ((), (), s32[]{:S(2)}) async-start(), calls=%async_computation.10 | async-start | bytes 3276800 | tf_op jit(solution)/shard_map/all_gather | solution.py:131
  47.8 1.9 copy-start.21
  47.9 1.9 copy-start.23
  51.1 132.0 %reduce-scatter.15.cloned.1.call-start = ((), (), s32[]{:S(2)}) async-start(), calls=%async_computation.12 | async-start | bytes 1638400
  51.2 21.4 %collective-permute-start.3 = (bf16[3,160,896]{2,1,0:T(8,128)(2,1)S(1)}, bf16[3,160,896]{2,1,0:T(8,128)(2,1)S(1)}, u32[]{:S(2)}, u32[]{:S(2)}) collective-permute-start(bf16[3,160,896]{2,1,0:T(8,128)(2,1)S(1)} %pad_maximum_fusion.5), channel_id=1, source_target_pairs={{0,24},{4,28},{8,0},{12,4},{16,8},{20,12},{24,16},{28,20},{1,25},{... | collective-permute-start | bytes 2580488 | tf_op jit(solution)/shard_map/ppermute | solution.py:51
  51.2 38.8 %collective-permute-start.2 = (bf16[3,160,896]{2,1,0:T(8,128)(2,1)S(1)}, bf16[3,160,896]{2,1,0:T(8,128)(2,1)S(1)}, u32[]{:S(2)}, u32[]{:S(2)}) collective-permute-start(bf16[3,160,896]{2,1,0:T(8,128)(2,1)S(1)} %pad_maximum_fusion.5), channel_id=1, source_target_pairs={{0,16},{4,20},{8,24},{12,28},{16,0},{20,4},{24,8},{28,12},{1,17},{... | collective-permute-start | bytes 2580488 | tf_op jit(solution)/shard_map/ppermute | solution.py:51
  51.3 38.6 %collective-permute-start.1 = (bf16[3,160,896]{2,1,0:T(8,128)(2,1)S(1)}, bf16[3,160,896]{2,1,0:T(8,128)(2,1)S(1)}, u32[]{:S(2)}, u32[]{:S(2)}) collective-permute-start(bf16[3,160,896]{2,1,0:T(8,128)(2,1)S(1)} %pad_maximum_fusion.5), channel_id=1, source_target_pairs={{0,8},{4,12},{8,16},{12,20},{16,24},{20,28},{24,0},{28,4},{1,9},{5... | collective-permute-start | bytes 2580488 | tf_op jit(solution)/shard_map/ppermute | solution.py:51
  72.5 19.7 %copy-start.3 = (bf16[3,160,896]{2,1,0:T(8,128)(2,1)}, bf16[3,160,896]{2,1,0:T(8,128)(2,1)S(1)}, u32[]{:S(2)}) copy-start(bf16[3,160,896]{2,1,0:T(8,128)(2,1)S(1)} %collective-permute-done.3) | copy-start | bytes 2580484
  90.0 2.2 copy-start.5
  90.0 2.3 copy-start.7
  90.0 3.6 copy-start.22
  92.2 17.4 %collective-permute-start.4 = (bf16[4,3,160,896]{3,2,0,1:T(8,128)(2,1)}, bf16[4,3,160,896]{3,2,0,1:T(8,128)(2,1)}, u32[]{:S(2)}, u32[]{:S(2)}) collective-permute-start(bf16[4,3,160,896]{3,2,0,1:T(8,128)(2,1)} %pad_maximum_fusion.1), channel_id=1, source_target_pairs={{0,4},{4,0},{8,12},{12,8},{16,20},{20,16},{24,28},{28,24},{1,5},{5... | collective-permute-start | bytes 10321928 | tf_op jit(solution)/shard_map/ppermute | solution.py:53
  109.0 1.9 copy-start.8
  109.6 9.8 %copy-start.9 = (bf16[1024,1280]{0,1:T(8,128)(2,1)}, bf16[1024,1280]{0,1:T(8,128)(2,1)S(1)}, u32[]{:S(2)}) copy-start(bf16[1024,1280]{0,1:T(8,128)(2,1)S(1)} %fusion.11) | copy-start | bytes 7864324
  115.3 3.0 copy-start.28
  121.4 11.5 %collective-permute-start.5 = (bf16[2,512,320]{1,2,0:T(8,128)(2,1)}, bf16[2,512,320]{1,2,0:T(8,128)(2,1)}, u32[]{:S(2)}, u32[]{:S(2)}) collective-permute-start(bf16[2,512,320]{1,2,0:T(8,128)(2,1)} %pad_maximum_fusion.8), channel_id=1, source_target_pairs={{0,4},{4,8},{8,12},{12,16},{16,20},{20,24},{24,28},{1,5},{5,9},{9,... | collective-permute-start | bytes 1966088 | tf_op jit(solution)/shard_map/ppermute | solution.py:14
  129.4 4.6 copy-start.11
  144.3 6.0 %copy-start.30 = (bf16[320,1280]{1,0:T(8,128)(2,1)S(1)}, bf16[320,1280]{1,0:T(8,128)(2,1)}, u32[]{:S(2)}) copy-start(bf16[320,1280]{1,0:T(8,128)(2,1)} %param.29) | copy-start | bytes 2457604
  152.3 63.1 %reduce-scatter.13.cloned.1.call-start = ((), (), s32[]{:S(2)}) async-start(), calls=%async_computation.11 | async-start | bytes 1638400
  163.1 5.9 %copy-start.31 = (bf16[320,1280]{1,0:T(8,128)(2,1)S(1)}, bf16[320,1280]{1,0:T(8,128)(2,1)}, u32[]{:S(2)}) copy-start(bf16[320,1280]{1,0:T(8,128)(2,1)} %param.29) | copy-start | bytes 2457604
  171.0 78.5 %all-gather.9.cloned.1.call-start = ((), (), s32[]{:S(2)}) async-start(), calls=%async_computation.7 | async-start | bytes 1638400 | tf_op jit(solution)/shard_map/all_gather | solution.py:196
  185.5 97.5 %all-gather.7.cloned.1.call-start = ((), (), s32[]{:S(2)}) async-start(), calls=%async_computation.6 | async-start | bytes 1638400 | tf_op jit(solution)/shard_map/all_gather | solution.py:196
  217.8 96.6 %reduce-scatter.19.cloned.1.call-start = ((), (), s32[]{:S(2)}) async-start(), calls=%async_computation.14 | async-start | bytes 1638400
  262.1 84.7 %reduce-scatter.17.cloned.1.call-start = ((), (), s32[]{:S(2)}) async-start(), calls=%async_computation.13 | async-start | bytes 1638400
  295.6 85.5 %all-gather.13.cloned.1.call-start = ((), (), s32[]{:S(2)}) async-start(), calls=%async_computation.9 | async-start | bytes 1638400 | tf_op jit(solution)/shard_map/all_gather | solution.py:220
  317.5 31.7 %copy-start.24 = (s32[32]{0:T(128)S(1)}, s32[32]{0:T(128)}, u32[]{:S(2)}) copy-start(s32[32]{0:T(128)} %param.22) | copy-start | bytes 388
  319.5 95.1 %all-gather.11.cloned.1.call-start = ((), (), s32[]{:S(2)}) async-start(), calls=%async_computation.8 | async-start | bytes 1638400 | tf_op jit(solution)/shard_map/all_gather | solution.py:220
  349.2 68.8 %collective-permute-start = (s32[1]{0:T(128)S(1)}, s32[1]{0:T(128)}, u32[]{:S(2)}, u32[]{:S(2)}) collective-permute-start(s32[1]{0:T(128)S(1)} %bitcast.153), channel_id=1, source_target_pairs={{4,0},{8,4},{12,8},{16,12},{20,16},{24,20},{28,24},{5,1},{9,5},{13... | collective-permute-start | bytes 20 | tf_op jit(solution)/shard_map/ppermute | solution.py:14
  381.0 3.0 copy-start.25
  414.6 28.8 %collective-permute-start.6 = (bf16[512,1280]{0,1:T(8,128)(2,1)}, bf16[512,1280]{0,1:T(8,128)(2,1)S(1)}, u32[]{:S(2)}, u32[]{:S(2)}) collective-permute-start(bf16[512,1280]{0,1:T(8,128)(2,1)} %all-gather.11.cloned.1.call-done), channel_id=1, source_target_pairs={{0,4},{4,8},{8,12},{12,16},{16,20},{20,24},{24,28},{1,5},{5,9},{9,... | collective-permute-start | bytes 3932168 | tf_op jit(solution)/shard_map/ppermute | solution.py:25
  418.7 5.4 %copy-start.27 = (bf16[512,1280]{0,1:T(8,128)(2,1)S(1)}, bf16[512,1280]{0,1:T(8,128)(2,1)}, u32[]{:S(2)}) copy-start(bf16[512,1280]{0,1:T(8,128)(2,1)} %all-gather.11.cloned.1.call-done) | copy-start | bytes 3932164
  418.8 29.7 %collective-permute-start.7 = (bf16[512,1280]{0,1:T(8,128)(2,1)S(1)}, bf16[512,1280]{0,1:T(8,128)(2,1)S(1)}, u32[]{:S(2)}, u32[]{:S(2)}) collective-permute-start(bf16[512,1280]{0,1:T(8,128)(2,1)S(1)} %copy-done.25), channel_id=1, source_target_pairs={{4,0},{8,4},{12,8},{16,12},{20,16},{24,20},{28,24},{5,1},{9,5},{13... | collective-permute-start | bytes 3932168 | tf_op jit(solution)/shard_map/ppermute | solution.py:27
  426.5 22.1 %copy-start.32 = (bf16[1280,320]{0,1:T(8,128)(2,1)S(1)}, bf16[1280,320]{0,1:T(8,128)(2,1)}, u32[]{:S(2)}) copy-start(bf16[1280,320]{0,1:T(8,128)(2,1)} %param.35) | copy-start | bytes 2457604
  452.2 1.6 copy-start.13
  452.2 2.1 copy-start.16
  453.8 1.6 copy-start.14
  455.5 1.8 copy-start.15
  455.5 1.8 copy-start.17
  458.5 3.0 copy-start.12
  458.5 15.0 %copy-start.1 = (bf16[4096,320]{0,1:T(8,128)(2,1)S(1)}, bf16[4096,320]{0,1:T(8,128)(2,1)}, u32[]{:S(2)}) copy-start(bf16[4096,320]{0,1:T(8,128)(2,1)} %param.24) | copy-start | bytes 7864324
  461.7 3.5 collective-permute-start.10
  462.4 8.1 %collective-permute-start.9 = (bf16[32,1280]{1,0:T(8,128)(2,1)S(1)}, bf16[32,1280]{1,0:T(8,128)(2,1)S(1)}, u32[]{:S(2)}, u32[]{:S(2)}) collective-permute-start(bf16[32,1280]{1,0:T(8,128)(2,1)S(1)} %convolution_convert_fusion.4), channel_id=1, source_target_pairs={{0,2},{1,3},{2,0},{3,1},{4,6},{5,7},{6,4},{7,5},{8,10},{9,11},{10,... | collective-permute-start | bytes 245768 | tf_op jit(solution)/shard_map/ppermute | solution.py:287
  462.7 7.8 %collective-permute-start.8 = (bf16[32,1280]{1,0:T(8,128)(2,1)S(1)}, bf16[32,1280]{1,0:T(8,128)(2,1)S(1)}, u32[]{:S(2)}, u32[]{:S(2)}) collective-permute-start(bf16[32,1280]{1,0:T(8,128)(2,1)S(1)} %convolution_convert_fusion.4), channel_id=1, source_target_pairs={{0,1},{1,2},{2,3},{3,0},{4,5},{5,6},{6,7},{7,4},{8,9},{9,10},{10,1... | collective-permute-start | bytes 245768 | tf_op jit(solution)/shard_map/ppermute | solution.py:287
  (7 other events, 8.3 us)
Sparse Core Ops, SparseCore 0:
  51.2 54.8 all-gather.14
  152.4 30.5 reduce-scatter.14
  185.4 29.9 reduce-scatter.12
  216.8 32.6 all-gather.8
  250.9 31.9 all-gather.6
  285.1 29.3 reduce-scatter.18
  316.8 29.9 reduce-scatter.16
  348.4 32.6 all-gather.12
  382.6 31.9 all-gather.10

commit v4 on v1

--- a/solution.py
+++ b/solution.py
@@ -40,6 +40,29 @@
     highest = jnp.max(scores, axis=-1, keepdims=True)
     raised = jnp.exp(scores - highest)
     return raised / jnp.sum(raised, axis=-1, keepdims=True)
+
+
+def spread_weights(own):
+    count = lax.axis_size("seq")
+    near = [own]
+    for step in range(1, count // 2):
+        near.append(lax.ppermute(own, "seq", [(i, (i + 2 * step) % count) for i in range(count)]))
+    near = jnp.stack(near)
+    return near, lax.ppermute(near, "seq", [(i, i ^ 1) for i in range(count)])
+
+
+def ordered_weights(near, far):
+    position = lax.axis_index("seq")
+    pairs, parts, rows, width = near.shape
+    even = position % 2 == 0
+    both = jnp.stack([jnp.where(even, near, far), jnp.where(even, far, near)], axis=1)
+    ordered = jnp.stack(
+        [
+            lax.dynamic_index_in_dim(both, (position // 2 - i) % pairs, keepdims=False)
+            for i in range(pairs)
+        ]
+    )
+    return [ordered[:, :, part].reshape(pairs * 2 * rows, width) for part in range(parts)]
 
 
 def per_device(
@@ -98,12 +121,9 @@
     )
     byte_rows = jnp.dot(byte_hot, byte_table, preferred_element_type=jnp.float32)
     embed = (byte_rows + hash_rows).astype(jnp.bfloat16)
-    full_gate = lax.all_gather(w_gate, "seq", axis=0, tiled=True)
-    full_up = lax.all_gather(w_up, "seq", axis=0, tiled=True)
-    full_down = lax.all_gather(w_down, "seq", axis=1, tiled=True)
-    embed, full_gate, full_up, full_down = lax.optimization_barrier(
-        (embed, full_gate, full_up, full_down)
-    )
+    packed = jnp.stack([w_gate, w_up, w_down.T])
+    embed, packed = lax.optimization_barrier((embed, packed))
+    near, far = spread_weights(packed)
     embed_parts = lax.all_gather(embed, "mp", axis=0, tiled=False)
     embed_full = jnp.concatenate(
         [embed_parts[i] for i in range(embed_parts.shape[0])], axis=1
@@ -148,11 +168,13 @@
         ).astype(jnp.bfloat16)
         outputs.append(mixed_block.reshape(WINDOW, local_width))
     heads_out = jnp.concatenate(outputs, axis=0)
+    attn_terms = jnp.dot(heads_out, w_attn_out, preferred_element_type=jnp.float32).astype(
+        jnp.bfloat16
+    )
+    near, far, _ = lax.optimization_barrier((near, far, attn_terms))
+    full_gate, full_up, full_down = ordered_weights(near, far)
     residual = residual + lax.psum_scatter(
-        jnp.dot(heads_out, w_attn_out, preferred_element_type=jnp.float32).astype(jnp.bfloat16),
-        "mp",
-        scatter_dimension=0,
-        tiled=True,
+        attn_terms, "mp", scatter_dimension=0, tiled=True
     ).astype(jnp.float32)
     normed = rms_scale(residual, norm_gains[1]).astype(jnp.bfloat16)
     mlp_in = lax.all_gather(normed, "mp", axis=0, tiled=True)
@@ -165,10 +187,8 @@
         mlp_in, full_up, preferred_element_type=jnp.float32
     )
     hidden = (jax.nn.silu(gate) * lifted).astype(jnp.bfloat16)
-    down_terms = jnp.dot(
-        hidden,
-        full_down,
-        preferred_element_type=jnp.float32,
+    down_terms = lax.dot_general(
+        hidden, full_down, (((1,), (1,)), ((), ())), preferred_element_type=jnp.float32
     )
     residual = residual + lax.psum_scatter(
         down_terms.astype(jnp.bfloat16), "mp", scatter_dimension=0, tiled=True

time: 527 us -> 469 us (0.89)
  waiting for transfers between devices: 345 us -> 297 us
  blocking collectives: 32.3 us -> 7.56 us
  matrix products: 81.6 us -> 89.2 us
  starting transfers between devices: 14.6 us -> 20.9 us
    all_gather x3 -> x0, waiting for transfers between devices: 54.2 us -> none  [the longest x1 30.7 us: per_device(): full_down = lax.all_gather(w_down, 'seq', axis=1, tiled=True)]
    reduce_scatter x1, waiting for transfers between devices: 49.3 us -> 7.19 us  [per_device(): lax.psum_scatter(attn_terms, 'mp', scatter_dimension=0, tiled=True)]
    ppermute x0 -> x4, waiting for transfers between devices: none -> 39 us  [the longest x3 39 us: spread_weights(): lax.ppermute(own, 'seq', [(i, (i + 2 * step) % count) for i in range(coun...]
    all_to_all x1 -> x0, blocking collectives: 24.6 us -> none  [per_device(): lax.all_to_all(found.reshape(seq_count, capacity, -1), 'seq', split_axis=...]
    all_to_all x0 -> x1, waiting for transfers between devices: none -> 16.5 us  [per_device(): lax.all_to_all(found.reshape(seq_count, capacity, -1), 'seq', split_axis=...]
    dot_general x1, matrix products: 3.06 us -> 11.6 us  [per_device(): jnp.dot(heads_out, w_attn_out, preferred_element_type=jnp.float32)]
    all_gather x1, waiting for transfers between devices: 55 us -> 47.5 us  [per_device(): mlp_in = lax.all_gather(normed, 'mp', axis=0, tiled=True)]
    another operation x1 -> x6, other arithmetic: 0.7 us -> 6.96 us  [the longest x2 3.51 us: ordered_weights(): jnp.stack([jnp.where(even, near, far), jnp.where(even, far, near)], axis=1)]
  transfers between devices with their start and end apart: 15 -> 17, of which waited for: 12 -> 14; matrix products, arithmetic and copies ran while one was open for 7% -> 8% of each run, Pallas kernels for 0% -> 0%
where the time goes in v4:
time: 469 us; the launch traced here: 464 us
  waiting for transfers between devices  297 us (63%)
  matrix products  89.2 us (19%)
  other arithmetic  23 us (5%)
  starting transfers between devices  20.9 us (4%)
  between operations  14.7 us (3%)
  local copies, waits for them, and re-layouts  11.5 us (2%)
  blocking collectives  7.56 us (2%)
    all_gather x1, waiting for transfers between devices, per_device(): embed_parts = lax.all_gather(embed, 'mp', axis=0, tiled=False)  51.9 us
    reduce_scatter x1, waiting for transfers between devices, per_device(): lax.psum_scatter(down_terms.astype(jnp.bfloat16), 'mp', scatter_dimension...  49.8 us
    all_gather x1, waiting for transfers between devices, per_device(): states = lax.all_gather(encoded, 'mp', axis=0, tiled=True)  48.6 us
    all_gather x1, waiting for transfers between devices, per_device(): mlp_in = lax.all_gather(normed, 'mp', axis=0, tiled=True)  47.5 us
    ppermute x3, waiting for transfers between devices, spread_weights(): lax.ppermute(own, 'seq', [(i, (i + 2 * step) % count) for i in range(coun...  39 us
    ppermute x1, waiting for transfers between devices, padded(): lax.ppermute(tail, axis, [(i, (i + 1) % count) for i in range(ends)])  20.9 us
    sub x2, matrix products, masked_softmax(): raised = jnp.exp(scores - highest)  17.5 us
    all_to_all x1, waiting for transfers between devices, per_device(): lax.all_to_all(found.reshape(seq_count, capacity, -1), 'seq', split_axis=...  16.5 us
  transfers between devices with their start and end apart: 17, of which 14 were waited for; matrix products, arithmetic and copies ran while one was open for 8% of the time, Pallas kernels for 0%

profile of v4, /device:TPU:3, one launch (start us, length us, event | category | flops | bytes accessed | tf_op | source)
XLA Modules:
  0.0 463.7 jit_solution(16990141248146565698)
XLA Ops:
  6.5 1.3 fusion.50
  9.3 1.6 fusion.40
  10.9 7.6 %all_to_all.11 = s32[8,1,256]{2,1,0:T(1,128)S(1)} all-to-all(s32[8,1,256]{2,1,0:T(1,128)S(1)} %bitcast.121), channel_id=1, replica_groups=mesh['seq'=8,'mp'=4] {'seq'}, dimensions={0} | all-to-all | bytes 16384 | tf_op jit(solution)/shard_map/all_to_all | solution.py:110
  18.5 6.4 %fusion.33 = bf16[2048,320]{0,1:T(8,128)(2,1)S(1)} fusion(bf16[4096,320]{0,1:T(8,128)(2,1)S(1)} %copy-done, s32[2048]{0:T(1024)S(1)} %bitcast.123), kind=kOutput, calls=%fused_computation.57 | convolution fusion | flops 5377753088 | bytes 3940352 | tf_op jit(solution)/shard_map/dot_general | solution.py:114
  26.1 5.0 %all-to-all-start.1 = ((bf16[8,256,320]{1,2,0:T(8,128)(2,1)}), bf16[8,256,320]{1,2,0:T(8,128)(2,1)S(1)}, u32[]{:S(2)}, u32[]{:S(2)}) async-start(bf16[8,256,320]{1,2,0:T(8,128)(2,1)} %bitcast.96), calls=%async_computation.1 | async-start | bytes 2621440 | tf_op jit(solution)/shard_map/all_to_all | solution.py:115
  31.2 16.5 %all-to-all-done.1 = bf16[8,256,320]{1,2,0:T(8,128)(2,1)S(1)} async-done(((bf16[8,256,320]{1,2,0:T(8,128)(2,1)}), bf16[8,256,320]{1,2,0:T(8,128)(2,1)S(1)}, u32[]{:S(2)}, u32[]{:S(2)}) %all-to-all-start.1) | async-done | bytes 1310752 | tf_op jit(solution)/shard_map/all_to_all | solution.py:115
  47.9 1.9 fusion.5
  49.8 1.3 fusion.45
  51.5 1.3 and_and_fusion.1
  52.9 1.4 and_and_fusion
  54.2 51.9 %all-gather.9.cloned.1.call-done = bf16[4096,320]{0,1:T(8,128)(2,1)} async-done(((bf16[1024,320]{0,1:T(8,128)(2,1)}), bf16[4096,320]{0,1:T(8,128)(2,1)}) %all-gather.9.cloned.1.call-update) | async-done | bytes 2621456 | tf_op jit(solution)/shard_map/all_gather | solution.py:127
  106.2 1.9 fusion.80
  112.2 3.7 collective-permute-start.1
  118.0 8.7 %fusion.84 = (f32[5,512]{1,0:T(8,128)S(1)}, f32[5,512,1024]{2,1,0:T(8,128)}) fusion(pred[512,1024]{1,0:T(8,128)(4,1)} %and_and_fusion, bf16[512,5,64]{0,2,1:T(8,128)(2,1)} %bitcast.117, bf16[1024,5,64]{0,2,1:T(8,128)(2,1)S(1)} %bitcast.102), kind=kOutput, calls=%fused_computation.167 | convolution fusion | flops 346031104 | bytes 12003328 | tf_op jit(solution)/shard_map/sub | solution.py:41
  126.7 6.5 %fusion.46 = bf16[5,64,512]{2,1,0:T(8,128)(2,1)} fusion(bf16[1024,5,64]{0,2,1:T(8,128)(2,1)S(1)} %bitcast.104, f32[5,512,1024]{2,1,0:T(8,128)} %get-tuple-element.44, f32[5,512]{1,0:T(8,128)S(1)} %get-tuple-element.43), kind=kOutput, calls=%fused_computation.91 | convolution fusion | flops 340951040 | bytes 11479040 | tf_op jit(solution)/shard_map/hqk,khd->qhd/dot_general | solution.py:166
  133.4 8.8 %fusion.85 = (f32[5,512]{1,0:T(8,128)S(1)}, f32[5,512,1024]{2,1,0:T(8,128)}) fusion(pred[512,1024]{1,0:T(8,128)(4,1)} %and_and_fusion.1, bf16[512,5,64]{0,2,1:T(8,128)(2,1)} %bitcast.116, bf16[1024,5,64]{0,2,1:T(8,128)(2,1)S(1)} %bitcast.115), kind=kOutput, calls=%fused_computation.168 | convolution fusion | flops 346031104 | bytes 12003328 | tf_op jit(solution)/shard_map/sub | solution.py:41
  142.2 5.9 %fusion.47 = bf16[5,64,512]{2,1,0:T(8,128)(2,1)S(1)} fusion(bf16[1024,5,64]{0,2,1:T(8,128)(2,1)S(1)} %bitcast.114, f32[5,512,1024]{2,1,0:T(8,128)} %get-tuple-element.46, f32[5,512]{1,0:T(8,128)S(1)} %get-tuple-element.45), kind=kOutput, calls=%fused_computation.92 | convolution fusion | flops 340951040 | bytes 11479040 | tf_op jit(solution)/shard_map/hqk,khd->qhd/dot_general | solution.py:166
  148.1 11.6 %convolution_convert_fusion.1 = bf16[1024,1280]{0,1:T(8,128)(2,1)} fusion(bf16[320,1280]{1,0:T(8,128)(2,1)S(1)} %copy-done.20, bf16[512,320]{0,1:T(8,128)(2,1)S(1)} %bitcast.128, bf16[512,320]{0,1:T(8,128)(2,1)S(1)} %bitcast.129), kind=kOutput, calls=%fused_computation.52 | convolution fusion | flops 841482240 | bytes 4096000 | tf_op jit(solution)/shard_map/dot_general | solution.py:171
  161.4 19.6 %collective-permute-done.2 = bf16[3,160,896]{2,1,0:T(8,128)(2,1)S(1)} collective-permute-done((bf16[3,160,896]{2,1,0:T(8,128)(2,1)S(1)}, bf16[3,160,896]{2,1,0:T(8,128)(2,1)S(1)}, u32[]{:S(2)}, u32[]{:S(2)}) %collective-permute-start.2) | collective-permute-done | bytes 860192 | tf_op jit(solution)/shard_map/ppermute | solution.py:49
  181.0 19.4 %collective-permute-done.3 = bf16[3,160,896]{2,1,0:T(8,128)(2,1)S(1)} collective-permute-done((bf16[3,160,896]{2,1,0:T(8,128)(2,1)S(1)}, bf16[3,160,896]{2,1,0:T(8,128)(2,1)S(1)}, u32[]{:S(2)}, u32[]{:S(2)}) %collective-permute-start.3) | collective-permute-done | bytes 860192 | tf_op jit(solution)/shard_map/ppermute | solution.py:49
  200.4 1.6 pad_maximum_fusion.1
  202.0 7.2 %reduce-scatter.3.cloned.1.call-done = bf16[256,1280]{0,1:T(8,128)(2,1)} async-done(((bf16[1024,1280]{0,1:T(8,128)(2,1)}), bf16[256,1280]{0,1:T(8,128)(2,1)}) %reduce-scatter.3.cloned.1.call-update) | async-done | bytes 655376 | tf_op jit(solution)/shard_map/reduce_scatter | solution.py:176
  209.2 1.6 multiply_reduce_fusion.1
  210.8 2.4 multiply_convert_fusion.2
  213.3 2.6 select_bitcast_fusion
  218.0 2.8 fusion.78
  220.7 47.5 %all-gather.5.cloned.1.call-done = bf16[1024,1280]{0,1:T(8,128)(2,1)} async-done(((bf16[256,1280]{0,1:T(8,128)(2,1)}), bf16[1024,1280]{0,1:T(8,128)(2,1)}) %all-gather.5.cloned.1.call-update) | async-done | bytes 2621456 | tf_op jit(solution)/shard_map/all_gather | solution.py:180
  268.3 6.4 %fusion.87 = f32[1024,896]{1,0:T(8,128)} fusion(bf16[1024,1280]{0,1:T(8,128)(2,1)} %all-gather.5.cloned.1.call-done, bf16[1280,896]{1,0:T(8,128)(2,1)S(1)} %bitcast.107), kind=kOutput, calls=%fused_computation.170 | convolution fusion | flops 2348810240 | bytes 8585216 | tf_op jit(solution)/shard_map/dot_general | solution.py:181
  274.7 11.8 %convolution_convert_fusion = bf16[1024,1280]{0,1:T(8,128)(2,1)} fusion(bf16[1280,896]{1,0:T(8,128)(2,1)} %bitcast.106, f32[1024,896]{1,0:T(8,128)} %fusion.87, bf16[1024,1280]{0,1:T(8,128)(2,1)} %all-gather.5.cloned.1.call-done, bf16[1280,896]{1,0:T(8,128)(2,1)} %bitcast.105), kind=kOutput, calls=%fused_computation.51 | convolution fusion | flops 4704436224 | bytes 13500416 | tf_op jit(solution)/shard_map/dot_general | solution.py:190
  286.8 49.8 %reduce-scatter.5.cloned.1.call-done = bf16[256,1280]{0,1:T(8,128)(2,1)} async-done(((bf16[1024,1280]{0,1:T(8,128)(2,1)}), bf16[256,1280]{0,1:T(8,128)(2,1)}) %reduce-scatter.5.cloned.1.call-update) | async-done | bytes 655376 | tf_op jit(solution)/shard_map/reduce_scatter | solution.py:193
  336.6 1.4 multiply_reduce_fusion
  338.0 2.3 multiply_convert_fusion.1
  340.3 2.7 collective-permute-start
  343.2 3.1 collective-permute-done
  346.8 48.6 %all-gather.7.cloned.1.call-done = bf16[1024,1280]{0,1:T(8,128)(2,1)} async-done(((bf16[256,1280]{0,1:T(8,128)(2,1)}), bf16[1024,1280]{0,1:T(8,128)(2,1)}) %all-gather.7.cloned.1.call-update) | async-done | bytes 2621456 | tf_op jit(solution)/shard_map/all_gather | solution.py:197
  395.5 2.0 fusion.79
  397.5 3.4 collective-permute-start.6
  401.2 1.9 collective-permute-start.7
  405.5 20.9 %collective-permute-done.6 = bf16[512,1280]{0,1:T(8,128)(2,1)S(1)} collective-permute-done((bf16[512,1280]{0,1:T(8,128)(2,1)S(1)}, bf16[512,1280]{0,1:T(8,128)(2,1)S(1)}, u32[]{:S(2)}, u32[]{:S(2)}) %collective-permute-start.6) | collective-permute-done | bytes 1310752 | tf_op jit(solution)/shard_map/ppermute | solution.py:25
  426.6 4.6 collective-permute-done.7
  433.5 1.6 fusion.37
  436.4 1.4 fusion.36
  437.8 2.1 fusion.86
  441.2 2.8 fusion.48
  446.2 1.6 collective-permute-done.10
  447.8 2.8 collective-permute-done.8
  450.6 3.3 collective-permute-done.9
  453.9 3.0 convolution_convert_fusion.10
  (118 shorter events, 23.6 us)
Async XLA Ops:
  6.5 11.9 %copy-start = (bf16[4096,320]{0,1:T(8,128)(2,1)S(1)}, bf16[4096,320]{0,1:T(8,128)(2,1)}, u32[]{:S(2)}) copy-start(bf16[4096,320]{0,1:T(8,128)(2,1)} %param.24) | copy-start | bytes 7864324
  24.9 6.2 %copy-start.10 = (bf16[896,160]{0,1:T(8,128)(2,1)S(1)}, bf16[896,160]{0,1:T(8,128)(2,1)}, u32[]{:S(2)}) copy-start(bf16[896,160]{0,1:T(8,128)(2,1)} %param.32) | copy-start | bytes 860164
  24.9 6.2 %copy-start.11 = (bf16[160,896]{1,0:T(8,128)(2,1)S(1)}, bf16[160,896]{1,0:T(8,128)(2,1)}, u32[]{:S(2)}) copy-start(bf16[160,896]{1,0:T(8,128)(2,1)} %param.31) | copy-start | bytes 860164
  24.9 6.2 %copy-start.12 = (bf16[160,896]{1,0:T(8,128)(2,1)S(1)}, bf16[160,896]{1,0:T(8,128)(2,1)}, u32[]{:S(2)}) copy-start(bf16[160,896]{1,0:T(8,128)(2,1)} %param.30) | copy-start | bytes 860164
  26.1 21.6 %all-to-all-start.1 = ((bf16[8,256,320]{1,2,0:T(8,128)(2,1)}), bf16[8,256,320]{1,2,0:T(8,128)(2,1)S(1)}, u32[]{:S(2)}, u32[]{:S(2)}) async-start(bf16[8,256,320]{1,2,0:T(8,128)(2,1)} %bitcast.96), calls=%async_computation.1 | async-start | bytes 2621440 | tf_op jit(solution)/shard_map/all_to_all | solution.py:115
  31.0 75.1 %all-gather.9.cloned.1.call-start = ((), (), s32[]{:S(2)}) async-start(), calls=%async_computation.8 | async-start | bytes 3276800 | tf_op jit(solution)/shard_map/all_gather | solution.py:127
  31.2 130.1 %copy-start.5 = (bf16[3,160,896]{2,1,0:T(8,128)(2,1)}, bf16[3,160,896]{2,1,0:T(8,128)(2,1)S(1)}, u32[]{:S(2)}) copy-start(bf16[3,160,896]{2,1,0:T(8,128)(2,1)S(1)} %pad_maximum_fusion.5) | copy-start | bytes 2580484
  47.8 1.9 copy-start.13
  47.9 1.9 copy-start.15
  49.8 1.7 copy-start.14
  51.1 158.1 %reduce-scatter.3.cloned.1.call-start = ((), (), s32[]{:S(2)}) async-start(), calls=%async_computation.4 | async-start | bytes 3276800 | tf_op jit(solution)/shard_map/reduce_scatter | solution.py:176
  108.1 1.1 copy-start.17
  109.0 6.9 %copy-start.3 = (bf16[1024,1280]{0,1:T(8,128)(2,1)}, bf16[1024,1280]{0,1:T(8,128)(2,1)S(1)}, u32[]{:S(2)}) copy-start(bf16[1024,1280]{0,1:T(8,128)(2,1)S(1)} %get-tuple-element.17) | copy-start | bytes 7864324
  109.2 1.7 copy-start.18
  111.0 4.9 %copy-start.19 = (bf16[1280,320]{0,1:T(8,128)(2,1)S(1)}, bf16[1280,320]{0,1:T(8,128)(2,1)}, u32[]{:S(2)}) copy-start(bf16[1280,320]{0,1:T(8,128)(2,1)} %param.26) | copy-start | bytes 2457604
  112.2 21.0 %collective-permute-start.1 = (bf16[2,512,320]{1,2,0:T(8,128)(2,1)S(1)}, bf16[2,512,320]{1,2,0:T(8,128)(2,1)S(1)}, u32[]{:S(2)}, u32[]{:S(2)}) collective-permute-start(bf16[2,512,320]{1,2,0:T(8,128)(2,1)S(1)} %pad_maximum_fusion.8), channel_id=1, source_target_pairs={{0,4},{4,8},{8,12},{12,16},{16,20},{20,24},{24,28},{1,5},{5,9},{9,... | collective-permute-start | bytes 1966088 | tf_op jit(solution)/shard_map/ppermute | solution.py:14
  142.2 5.9 %copy-start.20 = (bf16[320,1280]{1,0:T(8,128)(2,1)S(1)}, bf16[320,1280]{1,0:T(8,128)(2,1)}, u32[]{:S(2)}) copy-start(bf16[320,1280]{1,0:T(8,128)(2,1)} %param.29) | copy-start | bytes 2457604
  142.2 5.9 %copy-start.24 = (bf16[5,64,512]{2,1,0:T(8,128)(2,1)S(1)}, bf16[5,64,512]{2,1,0:T(8,128)(2,1)}, u32[]{:S(2)}) copy-start(bf16[5,64,512]{2,1,0:T(8,128)(2,1)} %fusion.46) | copy-start | bytes 983044
  159.7 108.5 %all-gather.5.cloned.1.call-start = ((), (), s32[]{:S(2)}) async-start(), calls=%async_computation.5 | async-start | bytes 3276800 | tf_op jit(solution)/shard_map/all_gather | solution.py:180
  159.8 21.2 %collective-permute-start.2 = (bf16[3,160,896]{2,1,0:T(8,128)(2,1)S(1)}, bf16[3,160,896]{2,1,0:T(8,128)(2,1)S(1)}, u32[]{:S(2)}, u32[]{:S(2)}) collective-permute-start(bf16[3,160,896]{2,1,0:T(8,128)(2,1)S(1)} %pad_maximum_fusion.5), channel_id=1, source_target_pairs={{0,8},{4,12},{8,16},{12,20},{16,24},{20,28},{24,0},{28,4},{1,9},{5... | collective-permute-start | bytes 2580488 | tf_op jit(solution)/shard_map/ppermute | solution.py:49
  161.0 39.4 %collective-permute-start.3 = (bf16[3,160,896]{2,1,0:T(8,128)(2,1)S(1)}, bf16[3,160,896]{2,1,0:T(8,128)(2,1)S(1)}, u32[]{:S(2)}, u32[]{:S(2)}) collective-permute-start(bf16[3,160,896]{2,1,0:T(8,128)(2,1)S(1)} %pad_maximum_fusion.5), channel_id=1, source_target_pairs={{0,16},{4,20},{8,24},{12,28},{16,0},{20,4},{24,8},{28,12},{1,17},{... | collective-permute-start | bytes 2580488 | tf_op jit(solution)/shard_map/ppermute | solution.py:49
  161.3 39.1 %collective-permute-start.4 = (bf16[3,160,896]{2,1,0:T(8,128)(2,1)S(1)}, bf16[3,160,896]{2,1,0:T(8,128)(2,1)S(1)}, u32[]{:S(2)}, u32[]{:S(2)}) collective-permute-start(bf16[3,160,896]{2,1,0:T(8,128)(2,1)S(1)} %pad_maximum_fusion.5), channel_id=1, source_target_pairs={{0,24},{4,28},{8,0},{12,4},{16,8},{20,12},{24,16},{28,20},{1,25},{... | collective-permute-start | bytes 2580488 | tf_op jit(solution)/shard_map/ppermute | solution.py:49
  201.9 11.4 %collective-permute-start.5 = (bf16[4,3,160,896]{3,2,0,1:T(8,128)(2,1)S(1)}, bf16[4,3,160,896]{3,2,0,1:T(8,128)(2,1)}, u32[]{:S(2)}, u32[]{:S(2)}) collective-permute-start(bf16[4,3,160,896]{3,2,0,1:T(8,128)(2,1)S(1)} %pad_maximum_fusion.1), channel_id=1, source_target_pairs={{0,4},{4,0},{8,12},{12,8},{16,20},{20,16},{24,28},{28,24},{1,5},{5... | collective-permute-start | bytes 10321928 | tf_op jit(solution)/shard_map/ppermute | solution.py:51
  213.2 123.4 %reduce-scatter.5.cloned.1.call-start = ((), (), s32[]{:S(2)}) async-start(), calls=%async_computation.6 | async-start | bytes 3276800 | tf_op jit(solution)/shard_map/reduce_scatter | solution.py:193
  274.7 61.9 %copy-start.4 = (bf16[1024,1280]{0,1:T(8,128)(2,1)S(1)}, bf16[1024,1280]{0,1:T(8,128)(2,1)}, u32[]{:S(2)}) copy-start(bf16[1024,1280]{0,1:T(8,128)(2,1)} %copy-done.3) | copy-start | bytes 7864324
  286.5 50.1 %copy-start.2 = (bf16[256,1280]{0,1:T(8,128)(2,1)S(1)}, bf16[256,1280]{0,1:T(8,128)(2,1)}, u32[]{:S(2)}) copy-start(bf16[256,1280]{0,1:T(8,128)(2,1)} %reduce-scatter.3.cloned.1.call-done) | copy-start | bytes 1966084
  286.5 53.8 %copy-start.16 = (s32[32]{0:T(128)S(1)}, s32[32]{0:T(128)}, u32[]{:S(2)}) copy-start(s32[32]{0:T(128)} %param.22) | copy-start | bytes 388
  286.5 108.9 %all-gather.7.cloned.1.call-start = ((), (), s32[]{:S(2)}) async-start(), calls=%async_computation.7 | async-start | bytes 3276800 | tf_op jit(solution)/shard_map/all_gather | solution.py:197
  340.3 5.9 %collective-permute-start = (s32[1]{0:T(128)S(1)}, s32[1]{0:T(128)}, u32[]{:S(2)}, u32[]{:S(2)}) collective-permute-start(s32[1]{0:T(128)S(1)} %bitcast.127), channel_id=1, source_target_pairs={{4,0},{8,4},{12,8},{16,12},{20,16},{24,20},{28,24},{5,1},{9,5},{13... | collective-permute-start | bytes 20 | tf_op jit(solution)/shard_map/ppermute | solution.py:14
  346.8 56.5 %copy-start.21 = (bf16[1280,320]{0,1:T(8,128)(2,1)S(1)}, bf16[1280,320]{0,1:T(8,128)(2,1)}, u32[]{:S(2)}) copy-start(bf16[1280,320]{0,1:T(8,128)(2,1)} %param.34) | copy-start | bytes 2457604
  395.5 7.8 %copy-start.6 = (bf16[1024,1280]{0,1:T(8,128)(2,1)S(1)}, bf16[1024,1280]{0,1:T(8,128)(2,1)}, u32[]{:S(2)}) copy-start(bf16[1024,1280]{0,1:T(8,128)(2,1)} %all-gather.7.cloned.1.call-done) | copy-start | bytes 7864324
  397.5 28.9 %collective-permute-start.6 = (bf16[512,1280]{0,1:T(8,128)(2,1)S(1)}, bf16[512,1280]{0,1:T(8,128)(2,1)S(1)}, u32[]{:S(2)}, u32[]{:S(2)}) collective-permute-start(bf16[512,1280]{0,1:T(8,128)(2,1)S(1)} %get-tuple-element.27), channel_id=1, source_target_pairs={{0,4},{4,8},{8,12},{12,16},{16,20},{20,24},{24,28},{1,5},{5,9},{9,... | collective-permute-start | bytes 3932168 | tf_op jit(solution)/shard_map/ppermute | solution.py:25
  401.2 29.9 %collective-permute-start.7 = (bf16[512,1280]{0,1:T(8,128)(2,1)S(1)}, bf16[512,1280]{0,1:T(8,128)(2,1)S(1)}, u32[]{:S(2)}, u32[]{:S(2)}) collective-permute-start(bf16[512,1280]{0,1:T(8,128)(2,1)S(1)} %get-tuple-element.28), channel_id=1, source_target_pairs={{4,0},{8,4},{12,8},{16,12},{20,16},{24,20},{28,24},{5,1},{9,5},{13... | collective-permute-start | bytes 3932168 | tf_op jit(solution)/shard_map/ppermute | solution.py:27
  403.3 1.1 copy-start.23
  405.5 25.9 %copy-start.22 = (bf16[1280,320]{0,1:T(8,128)(2,1)S(1)}, bf16[1280,320]{0,1:T(8,128)(2,1)}, u32[]{:S(2)}) copy-start(bf16[1280,320]{0,1:T(8,128)(2,1)} %param.34) | copy-start | bytes 2457604
  433.4 2.3 copy-start.8
  435.1 0.7 copy-start.9
  441.1 3.0 copy-start.7
  441.2 15.7 %copy-start.1 = (bf16[4096,320]{0,1:T(8,128)(2,1)S(1)}, bf16[4096,320]{0,1:T(8,128)(2,1)}, u32[]{:S(2)}) copy-start(bf16[4096,320]{0,1:T(8,128)(2,1)} %param.24) | copy-start | bytes 7864324
  444.4 3.5 collective-permute-start.10
  444.6 6.0 %collective-permute-start.8 = (bf16[32,1280]{1,0:T(8,128)(2,1)S(1)}, bf16[32,1280]{1,0:T(8,128)(2,1)S(1)}, u32[]{:S(2)}, u32[]{:S(2)}) collective-permute-start(bf16[32,1280]{1,0:T(8,128)(2,1)S(1)} %convolution_convert_fusion.2), channel_id=1, source_target_pairs={{0,1},{1,2},{2,3},{3,0},{4,5},{5,6},{6,7},{7,4},{8,9},{9,10},{10,1... | collective-permute-start | bytes 245768 | tf_op jit(solution)/shard_map/ppermute | solution.py:260
  445.9 8.0 %collective-permute-start.9 = (bf16[32,1280]{1,0:T(8,128)(2,1)S(1)}, bf16[32,1280]{1,0:T(8,128)(2,1)S(1)}, u32[]{:S(2)}, u32[]{:S(2)}) collective-permute-start(bf16[32,1280]{1,0:T(8,128)(2,1)S(1)} %convolution_convert_fusion.2), channel_id=1, source_target_pairs={{0,2},{1,3},{2,0},{3,1},{4,6},{5,7},{6,4},{7,5},{8,10},{9,11},{10,... | collective-permute-start | bytes 245768 | tf_op jit(solution)/shard_map/ppermute | solution.py:260
Sparse Core Ops, SparseCore 0:
  51.2 54.8 all-gather.8
  159.8 49.3 reduce-scatter.2
  213.3 54.9 all-gather.4
  286.6 49.9 reduce-scatter.4
  340.4 54.9 all-gather.6
